TPU v7x, 256 devices: a whole 4x4x8 slice. The times are simulated.
256 devices in a mesh: dp: 16 (over z_lo, x), ctx: 16 (over z_hi, y, core).
Axes of the slice: x: 4, y: 4, z: 8 (z_hi: 2, z_lo: 4; z = z_hi * 4 + z_lo), core: 2. Of those that a mesh axis runs over, the one named last changes fastest.
Arguments:
- long_query: bfloat16 [16, 1536, 4096], P('dp', 'ctx'), may hold values from -5 to 5
- long_key: bfloat16 [16, 1536, 512], P('dp', 'ctx'), may hold values from -5 to 5
- long_value: bfloat16 [16, 1536, 512], P('dp', 'ctx'), may hold values from -6 to 6
- long_cotangent: bfloat16 [16, 1536, 4096], P('dp', 'ctx'), may hold values from -6 to 6
- block_order: int32 [16, 32], P('dp'), may hold values from 0 to 31, each once within a row
- short_query: bfloat16 [16, 1024, 4096], P('dp', 'ctx'), may hold values from -5 to 5
- short_key: bfloat16 [16, 1024, 512], P('dp', 'ctx'), may hold values from -5 to 5
- short_value: bfloat16 [16, 1024, 512], P('dp', 'ctx'), may hold values from -6 to 6
- short_cotangent: bfloat16 [16, 1024, 4096], P('dp', 'ctx'), may hold values from -6 to 6
- doc_lengths: int32 [16, 16, 4], P(None, 'ctx'), may hold values from 1 to 32, 64 in all within a row
- balance_list: int32 [16, 16], P('ctx'), may hold values from 0 to 15, as said below
Outputs:
- long_output: bfloat16 [16, 1536, 4096], P('dp', 'ctx')
- long_query_grad: bfloat16 [16, 1536, 4096], P('dp', 'ctx')
- long_key_grad: bfloat16 [16, 1536, 512], P('dp', 'ctx')
- long_value_grad: bfloat16 [16, 1536, 512], P('dp', 'ctx')
- short_output: bfloat16 [16, 1024, 4096], P('dp', 'ctx')
- short_query_grad: bfloat16 [16, 1024, 4096], P('dp', 'ctx')
- short_key_grad: bfloat16 [16, 1024, 512], P('dp', 'ctx')
- short_value_grad: bfloat16 [16, 1024, 512], P('dp', 'ctx')
Inputs may be any that keep to these rules, and one draw needn't show every extreme that they name: `block_order`: each row is a permutation of 0 to 31. `balance_list`: row c maps each data group j to j XOR m_c, for one number m_c of 0 to 15 per row; in some row m_c = 15, and in another row m_c = 8. `doc_lengths`: the lengths of a pack sum to 64; the longest is exactly 32.
All inputs are finite; a program needn't handle non-finite values.
Results may differ from a plain program's by a relative error of at most 0.012.
Values may be sent and summed in bfloat16 or wider, within the bound.
A program may use at most 128 MiB of HBM per device.

v0:
```python
import jax
import jax.numpy as jnp
from jax import lax
from jax.sharding import PartitionSpec as P

HD = 128
Q_HEADS = 32
KV_HEADS = 4


def attend(queries, keyset, valueset, cotangent, allowed):
    scale_factor = HD ** (-0.5)
    scores = (
        jnp.einsum("rgd,kd->grk", queries, keyset, preferred_element_type=jnp.float32)
        * scale_factor
    )
    masked = jnp.where(allowed[None], scores, -1e30)
    highest = jnp.max(masked, axis=2, keepdims=True)
    total = jnp.sum(jnp.exp(masked - highest), axis=2, keepdims=True)
    probs = jnp.exp(masked - highest - jnp.log(total))
    probs_low = probs.astype(jnp.bfloat16)
    output = jnp.einsum(
        "grk,kd->rgd", probs_low, valueset, preferred_element_type=jnp.float32
    ).astype(jnp.bfloat16)
    deltas = jnp.sum(
        cotangent.astype(jnp.float32) * lax.optimization_barrier(output).astype(jnp.float32), axis=2
    )
    dprobs = jnp.einsum("rgd,kd->grk", cotangent, valueset, preferred_element_type=jnp.float32)
    dscores = probs * (dprobs - jnp.transpose(deltas)[:, :, None])
    dscore_low = dscores.astype(jnp.bfloat16)
    query_grad = (
        jnp.einsum("grk,kd->rgd", dscore_low, keyset, preferred_element_type=jnp.float32)
        * scale_factor
    ).astype(jnp.bfloat16)
    return (output, query_grad, probs_low, dscore_low)


def key_value_grads(queries, cotangent, probs_low, dscore_low):
    scale_factor = HD ** (-0.5)
    key_grad = (
        jnp.einsum("grk,rgd->kd", dscore_low, queries, preferred_element_type=jnp.float32)
        * scale_factor
    )
    value_grad = jnp.einsum("grk,rgd->kd", probs_low, cotangent, preferred_element_type=jnp.float32)
    return (key_grad, value_grad)


def forward_heads(query_rows, key_rows, value_rows, cot_rows, allowed):
    group_size = Q_HEADS // KV_HEADS
    row_count = query_rows.shape[0]
    key_count = key_rows.shape[0]
    queries = query_rows.reshape(row_count, KV_HEADS, group_size, HD)
    cotangents = cot_rows.reshape(row_count, KV_HEADS, group_size, HD)
    key_heads = key_rows.reshape(key_count, KV_HEADS, HD)
    value_heads = value_rows.reshape(key_count, KV_HEADS, HD)
    outputs, query_grads, prob_list, dscore_list = ([], [], [], [])
    for head_group in range(KV_HEADS):
        output, query_grad, probs_low, dscore_low = attend(
            queries[:, head_group],
            key_heads[:, head_group],
            value_heads[:, head_group],
            cotangents[:, head_group],
            allowed,
        )
        outputs.append(output)
        query_grads.append(query_grad)
        prob_list.append(probs_low)
        dscore_list.append(dscore_low)
    output = jnp.stack(outputs, axis=1).reshape(row_count, Q_HEADS * HD)
    query_grad = jnp.stack(query_grads, axis=1).reshape(row_count, Q_HEADS * HD)
    return (output, query_grad, prob_list, dscore_list, queries, cotangents)


def per_device(
    long_query,
    long_key,
    long_value,
    long_cotangent,
    block_order,
    short_query,
    short_key,
    short_value,
    short_cotangent,
    doc_lengths,
    balance_list,
):
    kv_width = KV_HEADS * HD
    my_column = lax.axis_index("ctx")
    row_count = long_query.shape[1]
    block = row_count // 2
    all_keys, all_values = (
        lax.all_gather(long_key[0], "ctx", axis=0, tiled=True),
        lax.all_gather(long_value[0], "ctx", axis=0, tiled=True),
    )
    ordering = block_order[0]
    positions = (ordering[:, None] * block + jnp.arange(block, dtype=jnp.int32)[None, :]).reshape(
        -1
    )
    my_positions = lax.dynamic_slice_in_dim(positions, my_column * row_count, row_count)
    allowed = my_positions[:, None] >= positions[None, :]
    long_out, long_qgrad, prob_list, dscore_list, queries, cotangents = forward_heads(
        long_query[0], all_keys, all_values, long_cotangent[0], allowed
    )
    key_parts = []
    value_parts = []
    for key_head_group in range(KV_HEADS):
        probs_part = prob_list[key_head_group]
        dscore_part = dscore_list[key_head_group]
        key_key_grad, key_value_grad = key_value_grads(
            queries[:, key_head_group], cotangents[:, key_head_group], probs_part, dscore_part
        )
        key_parts.append(key_key_grad)
        value_parts.append(key_value_grad)
    key_block = jnp.stack(key_parts, axis=1).reshape(row_count * lax.axis_size("ctx"), kv_width)
    value_block = jnp.stack(value_parts, axis=1).reshape(row_count * lax.axis_size("ctx"), kv_width)
    summed = lax.psum_scatter(
        jnp.concatenate([key_block, value_block], axis=1), "ctx", scatter_dimension=0, tiled=True
    )
    long_kgrad = summed[:, :kv_width].astype(jnp.bfloat16)
    long_vgrad = summed[:, kv_width:].astype(jnp.bfloat16)
    my_row = lax.axis_index("dp")
    group_count = lax.axis_size("dp")
    short_rows = short_query.shape[1]
    targets = balance_list[0]
    source = jnp.sum(jnp.where(targets == my_row, jnp.arange(group_count, dtype=jnp.int32), 0))
    portion = (
        lax.all_gather(short_query[0], "dp", axis=0, tiled=True),
        lax.all_gather(short_key[0], "dp", axis=0, tiled=True),
        lax.all_gather(short_value[0], "dp", axis=0, tiled=True),
    )
    amount = portion[0].shape[0]
    global_rows = jnp.arange(amount, dtype=jnp.int32)
    chosen = (global_rows // short_rows == source)[:, None] & (
        (global_rows % short_rows)[:, None] == jnp.arange(short_rows, dtype=jnp.int32)[None, :]
    )
    picker = chosen.astype(jnp.bfloat16)
    received = tuple(
        (
            jnp.einsum("rs,rf->sf", picker, member, preferred_element_type=jnp.float32)
            for member in portion
        )
    )
    pack_query = received[0].astype(jnp.bfloat16)
    pack_key = received[1].astype(jnp.bfloat16)
    pack_value = received[2].astype(jnp.bfloat16)
    doc_sizes = lax.dynamic_index_in_dim(doc_lengths[:, 0, :], source, 0, keepdims=False)
    doc_ends = jnp.cumsum(doc_sizes)
    steps_rows = jnp.arange(short_rows, dtype=jnp.int32)
    doc_ids = jnp.sum((steps_rows[:, None] >= doc_ends[None, :]).astype(jnp.int32), axis=1)
    short_allowed = (doc_ids[:, None] == doc_ids[None, :]) & (
        steps_rows[:, None] >= steps_rows[None, :]
    )
    short_out, short_qgrad, short_probs, short_dscores, pack_heads, pack_cots = forward_heads(
        pack_query, pack_key, pack_value, short_cotangent[0], short_allowed
    )
    key_parts, value_parts = ([], [])
    for head_group in range(KV_HEADS):
        key_grad, value_grad = key_value_grads(
            pack_heads[:, head_group],
            pack_cots[:, head_group],
            short_probs[head_group],
            short_dscores[head_group],
        )
        key_parts.append(key_grad)
        value_parts.append(value_grad)
    short_kgrad = jnp.stack(key_parts, axis=1).reshape(short_rows, kv_width).astype(jnp.bfloat16)
    short_vgrad = jnp.stack(value_parts, axis=1).reshape(short_rows, kv_width).astype(jnp.bfloat16)
    return (
        long_out[None],
        long_qgrad[None],
        long_kgrad[None],
        long_vgrad[None],
        short_out[None],
        short_qgrad[None],
        short_kgrad[None],
        short_vgrad[None],
    )


def solution(mesh):
    return jax.shard_map(
        per_device,
        mesh=mesh,
        in_specs=(
            P("dp", "ctx", None),
            P("dp", "ctx", None),
            P("dp", "ctx", None),
            P("dp", "ctx", None),
            P("dp", None),
            P("dp", "ctx", None),
            P("dp", "ctx", None),
            P("dp", "ctx", None),
            P("dp", "ctx", None),
            P(None, "ctx", None),
            P("ctx", None),
        ),
        out_specs=(
            P("dp", "ctx", None),
            P("dp", "ctx", None),
            P("dp", "ctx", None),
            P("dp", "ctx", None),
            P("dp", "ctx", None),
            P("dp", "ctx", None),
            P("dp", "ctx", None),
            P("dp", "ctx", None),
        ),
        check_vma=False,
    )
```

profile of v0, /device:TPU:1, one launch (start us, length us, event | category | flops | bytes accessed | tf_op | source)
XLA Modules:
  0.0 540.0 jit_solution(13604507288096642554)
XLA Ops:
  14.9 59.4 %all-gather.11.cloned.1.call-done = bf16[1,1536,512]{2,1,0:T(8,128)(2,1)} async-done(((bf16[1,96,512]{2,1,0:T(8,128)(2,1)}), bf16[1,1536,512]{2,1,0:T(8,128)(2,1)}) %all-gather.11.cloned.1.call-update) | async-done | bytes 1572880 | tf_op jit(solution)/shard_map/all_gather | solution.py:92
  76.1 3.5 fusion.37
  79.6 7.3 %fusion.21 = f32[8,96,1536]{2,1,0:T(8,128)} fusion(f32[8,96,1536]{2,1,0:T(8,128)} %fusion.37), kind=kOutput, calls=%fused_computation.26 | output fusion | flops 1181951 | bytes 9437184 | tf_op jit(solution)/shard_map/reduce_sum | solution.py:19
  87.0 45.4 %all-gather.13.cloned.1.call-done = bf16[1,1536,512]{2,1,0:T(8,128)(2,1)} async-done(((bf16[1,96,512]{2,1,0:T(8,128)(2,1)}), bf16[1,1536,512]{2,1,0:T(8,128)(2,1)}) %all-gather.13.cloned.1.call-update) | async-done | bytes 1572880 | tf_op jit(solution)/shard_map/all_gather | solution.py:93
  134.6 5.3 fusion.92
  139.9 4.6 fusion.39
  144.5 5.3 fusion.98
  149.8 7.3 %fusion.19 = f32[8,96,1536]{2,1,0:T(8,128)} fusion(f32[8,96,1536]{2,1,0:T(8,128)} %fusion.39), kind=kOutput, calls=%fused_computation.22 | output fusion | flops 1181951 | bytes 9437184 | tf_op jit(solution)/shard_map/reduce_sum | solution.py:19
  157.1 4.6 fusion.38
  161.7 5.3 fusion.95
  167.0 7.3 %fusion.20 = f32[8,96,1536]{2,1,0:T(8,128)} fusion(f32[8,96,1536]{2,1,0:T(8,128)} %fusion.38), kind=kOutput, calls=%fused_computation.24 | output fusion | flops 1181951 | bytes 9437184 | tf_op jit(solution)/shard_map/reduce_sum | solution.py:19
  174.3 4.5 fusion.40
  178.8 6.2 %fusion.101 = bf16[8,96,128]{2,1,0:T(8,128)(2,1)} fusion(f32[8,96,1536]{2,1,0:T(8,128)} %fusion.40, bf16[1536,4,128]{0,2,1:T(8,128)(2,1)S(1)} %bitcast.592), kind=kOutput, calls=%fused_computation.114 | convolution fusion | flops 304449792 | bytes 10027008 | tf_op jit(solution)/shard_map/grk,kd->rgd/dot_general | solution.py:22
  185.0 5.2 fusion.18
  202.1 6.3 %convolution_bitcast_fusion.3 = f32[1536,1,128]{0,2,1:T(8,128)} fusion(f32[8,96,1536]{2,1,0:T(8,128)} %fusion.37, bf16[96,1,8,128]{3,2,1,0:T(8,128)(2,1)} %copy-done.10), kind=kOutput, calls=%fused_computation.65 | convolution fusion | flops 304351488 | bytes 5701632 | tf_op jit(solution)/shard_map/grk,rgd->kd/dot_general | solution.py:44
  208.4 6.3 %convolution_bitcast_fusion.1 = f32[1536,1,128]{0,2,1:T(8,128)} fusion(f32[8,96,1536]{2,1,0:T(8,128)} %fusion.39, bf16[96,1,8,128]{3,2,1,0:T(8,128)(2,1)S(1)} %copy-done.9), kind=kOutput, calls=%fused_computation.63 | convolution fusion | flops 304351488 | bytes 5701632 | tf_op jit(solution)/shard_map/grk,rgd->kd/dot_general | solution.py:44
  214.7 6.3 %convolution_bitcast_fusion.2 = f32[1536,1,128]{0,2,1:T(8,128)} fusion(f32[8,96,1536]{2,1,0:T(8,128)} %fusion.38, bf16[96,1,8,128]{3,2,1,0:T(8,128)(2,1)S(1)} %get-tuple-element.10), kind=kOutput, calls=%fused_computation.64 | convolution fusion | flops 304351488 | bytes 5701632 | tf_op jit(solution)/shard_map/grk,rgd->kd/dot_general | solution.py:44
  221.0 6.3 %convolution_bitcast_fusion = f32[1536,1,128]{0,2,1:T(8,128)} fusion(f32[8,96,1536]{2,1,0:T(8,128)} %fusion.40, bf16[96,1,8,128]{3,2,1,0:T(8,128)(2,1)S(1)} %get-tuple-element.11), kind=kOutput, calls=%fused_computation.62 | convolution fusion | flops 304351488 | bytes 5701632 | tf_op jit(solution)/shard_map/grk,rgd->kd/dot_general | solution.py:44
  231.7 6.6 %pad_maximum_fusion = f32[1536,1024]{1,0:T(8,128)} fusion(f32[1536,512]{1,0:T(8,128)} %copy.162, f32[1536,512]{1,0:T(8,128)} %copy.161), kind=kLoop, calls=%fused_computation.18 | loop fusion | flops 1572864 | bytes 12582912 | tf_op jit(solution)/shard_map/concatenate | solution.py:117
  249.2 32.2 %all-gather.17.cloned.1.call-done = bf16[1,1024,512]{2,1,0:T(8,128)(2,1)} async-done(((bf16[1,64,512]{2,1,0:T(8,128)(2,1)}), bf16[1,1024,512]{2,1,0:T(8,128)(2,1)}) %all-gather.17.cloned.1.call-update) | async-done | bytes 1048592 | tf_op jit(solution)/shard_map/all_gather | solution.py:128
  292.4 2.5 fusion.146
  298.1 115.4 %reduce-scatter.2.cloned.1.call-done = f32[96,1024]{1,0:T(8,128)} async-done(((f32[1536,1024]{1,0:T(8,128)}), f32[96,1024]{1,0:T(8,128)}) %reduce-scatter.2.cloned.1.call-update) | async-done | bytes 393232 | tf_op jit(solution)/shard_map/reduce_scatter | solution.py:116
  415.3 99.6 %all-gather.19.cloned.1.call-done = bf16[1,1024,4096]{2,1,0:T(8,128)(2,1)} async-done(((bf16[1,64,4096]{2,1,0:T(8,128)(2,1)}), bf16[1,1024,4096]{2,1,0:T(8,128)(2,1)}) %all-gather.19.cloned.1.call-update) | async-done | bytes 8388624 | tf_op jit(solution)/shard_map/all_gather | solution.py:127
  514.9 5.1 fusion.73
  (207 shorter events, 65.0 us)
Async XLA Ops:
  7.2 234.3 %copy-start = (s32[16,1,4]{0,2,1:T(4,128)S(1)}, s32[16,1,4]{0,2,1:T(4,128)}, u32[]{:S(2)}) copy-start(s32[16,1,4]{0,2,1:T(4,128)} %param.20) | copy-start | bytes 772
  7.2 67.2 %all-gather.11.cloned.1.call-start = ((), (), s32[]{:S(2)}) async-start(), calls=%async_computation.2 | async-start | bytes 1671168 | tf_op jit(solution)/shard_map/all_gather | solution.py:92
  7.9 124.4 %all-gather.13.cloned.1.call-start = ((), (), s32[]{:S(2)}) async-start(), calls=%async_computation.3 | async-start | bytes 1671168 | tf_op jit(solution)/shard_map/all_gather | solution.py:93
  8.7 236.6 %all-gather.15.cloned.1.call-start = ((), (), s32[]{:S(2)}) async-start(), calls=%async_computation.4 | async-start | bytes 1114112 | tf_op jit(solution)/shard_map/all_gather | solution.py:129
  9.4 272.0 %all-gather.17.cloned.1.call-start = ((), (), s32[]{:S(2)}) async-start(), calls=%async_computation.5 | async-start | bytes 1114112 | tf_op jit(solution)/shard_map/all_gather | solution.py:128
  10.0 403.6 %reduce-scatter.2.cloned.1.call-start = ((), (), s32[]{:S(2)}) async-start(), calls=%async_computation.1 | async-start | bytes 6684672 | tf_op jit(solution)/shard_map/reduce_scatter | solution.py:116
  11.1 65.0 %copy-start.30 = (pred[96,1536]{1,0:T(8,128)(4,1)}, pred[96,1536]{1,0:T(8,128)(4,1)S(1)}, u32[]{:S(2)}) copy-start(pred[96,1536]{1,0:T(8,128)(4,1)S(1)} %broadcast_compare_fusion) | copy-start | bytes 442372
  13.3 66.4 %copy-start.28 = (bf16[96,1,8,128]{3,2,1,0:T(8,128)(2,1)}, bf16[96,1,8,128]{3,2,1,0:T(8,128)(2,1)S(1)}, u32[]{:S(2)}) copy-start(bf16[96,1,8,128]{3,2,1,0:T(8,128)(2,1)S(1)} %get-tuple-element.12) | copy-start | bytes 589828
  13.3 126.6 %copy-start.24 = (bf16[96,1,8,128]{3,2,1,0:T(8,128)(2,1)}, bf16[96,1,8,128]{3,2,1,0:T(8,128)(2,1)S(1)}, u32[]{:S(2)}) copy-start(bf16[96,1,8,128]{3,2,1,0:T(8,128)(2,1)S(1)} %get-tuple-element.13) | copy-start | bytes 589828
  13.3 143.8 %copy-start.26 = (bf16[96,1,8,128]{3,2,1,0:T(8,128)(2,1)}, bf16[96,1,8,128]{3,2,1,0:T(8,128)(2,1)S(1)}, u32[]{:S(2)}) copy-start(bf16[96,1,8,128]{3,2,1,0:T(8,128)(2,1)S(1)} %get-tuple-element.14) | copy-start | bytes 589828
  14.9 175.7 %copy-start.10 = (bf16[96,1,8,128]{3,2,1,0:T(8,128)(2,1)}, bf16[96,1,8,128]{3,2,1,0:T(8,128)(2,1)S(1)}, u32[]{:S(2)}) copy-start(bf16[96,1,8,128]{3,2,1,0:T(8,128)(2,1)S(1)} %get-tuple-element.8) | copy-start | bytes 589828
  14.9 180.6 %copy-start.8 = (bf16[96,1,8,128]{3,2,1,0:T(8,128)(2,1)}, bf16[96,1,8,128]{3,2,1,0:T(8,128)(2,1)S(1)}, u32[]{:S(2)}) copy-start(bf16[96,1,8,128]{3,2,1,0:T(8,128)(2,1)S(1)} %get-tuple-element.9) | copy-start | bytes 589828
  139.8 50.4 %copy-start.14 = (bf16[8,96,128]{2,1,0:T(8,128)(2,1)}, bf16[8,96,128]{2,1,0:T(8,128)(2,1)S(1)}, u32[]{:S(2)}) copy-start(bf16[8,96,128]{2,1,0:T(8,128)(2,1)S(1)} %fusion.92) | copy-start | bytes 589828
  238.2 50.6 %copy-start.15 = (bf16[8,96,128]{2,1,0:T(8,128)(2,1)S(1)}, bf16[8,96,128]{2,1,0:T(8,128)(2,1)}, u32[]{:S(2)}) copy-start(bf16[8,96,128]{2,1,0:T(8,128)(2,1)} %copy-done.14) | copy-start | bytes 589828
  238.2 50.6 %copy-start.17 = (bf16[8,96,128]{2,1,0:T(8,128)(2,1)S(1)}, bf16[8,96,128]{2,1,0:T(8,128)(2,1)}, u32[]{:S(2)}) copy-start(bf16[8,96,128]{2,1,0:T(8,128)(2,1)} %copy-done.16) | copy-start | bytes 589828
  238.2 50.6 %copy-start.19 = (bf16[8,96,128]{2,1,0:T(8,128)(2,1)S(1)}, bf16[8,96,128]{2,1,0:T(8,128)(2,1)}, u32[]{:S(2)}) copy-start(bf16[8,96,128]{2,1,0:T(8,128)(2,1)} %copy-done.18) | copy-start | bytes 589828
  238.2 50.6 %copy-start.21 = (bf16[8,96,128]{2,1,0:T(8,128)(2,1)S(1)}, bf16[8,96,128]{2,1,0:T(8,128)(2,1)}, u32[]{:S(2)}) copy-start(bf16[8,96,128]{2,1,0:T(8,128)(2,1)} %fusion.101) | copy-start | bytes 589828
  238.3 276.6 %all-gather.19.cloned.1.call-start = ((), (), s32[]{:S(2)}) async-start(), calls=%async_computation.6 | async-start | bytes 8912896 | tf_op jit(solution)/shard_map/all_gather | solution.py:127
  241.8 48.6 %copy-start.2 = (bf16[8,96,1536]{2,1,0:T(8,128)(2,1)S(1)}, bf16[8,96,1536]{2,1,0:T(8,128)(2,1)}, u32[]{:S(2)}) copy-start(bf16[8,96,1536]{2,1,0:T(8,128)(2,1)} %copy-done.1) | copy-start | bytes 7077892
  415.3 105.0 %copy-start.36 = (bf16[64,1,128]{2,1,0:T(2,128)(2,1)S(1)}, bf16[64,1,128]{2,1,0:T(2,128)(2,1)}, u32[]{:S(2)}) copy-start(bf16[64,1,128]{2,1,0:T(2,128)(2,1)} %get-tuple-element.30) | copy-start | bytes 49156
  415.3 105.0 %copy-start.40 = (pred[64,64]{0,1:T(8,128)(4,1)S(1)}, pred[64,64]{0,1:T(8,128)(4,1)}, u32[]{:S(2)}) copy-start(pred[64,64]{0,1:T(8,128)(4,1)} %fusion.240) | copy-start | bytes 12292
  415.3 105.7 %copy-start.38 = (bf16[64,1,128]{2,1,0:T(2,128)(2,1)S(1)}, bf16[64,1,128]{2,1,0:T(2,128)(2,1)}, u32[]{:S(2)}) copy-start(bf16[64,1,128]{2,1,0:T(2,128)(2,1)} %get-tuple-element.26) | copy-start | bytes 49156
  415.3 106.0 %copy-start.37 = (bf16[64,1,128]{2,1,0:T(2,128)(2,1)S(1)}, bf16[64,1,128]{2,1,0:T(2,128)(2,1)}, u32[]{:S(2)}) copy-start(bf16[64,1,128]{2,1,0:T(2,128)(2,1)} %get-tuple-element.32) | copy-start | bytes 49156
  415.3 106.7 %copy-start.39 = (bf16[64,1,128]{2,1,0:T(2,128)(2,1)S(1)}, bf16[64,1,128]{2,1,0:T(2,128)(2,1)}, u32[]{:S(2)}) copy-start(bf16[64,1,128]{2,1,0:T(2,128)(2,1)} %get-tuple-element.28) | copy-start | bytes 49156
  (30 other events, 183.7 us)
Sparse Core Ops, SparseCore 0:
  10.8 63.5 all-gather.10
  77.1 55.2 all-gather.12
  134.1 66.1 all-gather.14
  202.0 79.3 all-gather.16
  285.7 127.8 reduce-scatter.1
  415.2 99.6 all-gather.18
where the time goes:
time: 545 us; the launch traced here: 540 us
  waiting for transfers between devices  355 us (65%)
  matrix products  91.8 us (17%)
  other arithmetic  43.3 us (8%)
  local copies, waits for them, and re-layouts  32.3 us (6%)
  between operations  17.3 us (3%)
    reduce_scatter x1, waiting for transfers between devices, per_device(): lax.psum_scatter(jnp.concatenate([key_block, value_block], axis=1), 'ctx'...  115 us
    all_gather x1, waiting for transfers between devices, per_device(): lax.all_gather(short_query[0], 'dp', axis=0, tiled=True)  99.6 us
    all_gather x1, waiting for transfers between devices, per_device(): lax.all_gather(long_key[0], 'ctx', axis=0, tiled=True)  59.4 us
    all_gather x1, waiting for transfers between devices, per_device(): lax.all_gather(long_value[0], 'ctx', axis=0, tiled=True)  45.4 us
    all_gather x1, waiting for transfers between devices, per_device(): lax.all_gather(short_key[0], 'dp', axis=0, tiled=True)  32.2 us
    reduce_sum x8, other arithmetic, attend(): total = jnp.sum(jnp.exp(masked - highest), axis=2, keepdims=True)  28.8 us
    dot_general x8, matrix products, key_value_grads(): jnp.einsum('grk,rgd->kd', probs_low, cotangent, preferred_element_type=jn...  26.2 us
    dot_general x8, matrix products, attend(): jnp.einsum('grk,kd->rgd', probs_low, valueset, preferred_element_type=jnp...  23.1 us
  transfers between devices with their start and end apart: 6, of which 5 were waited for; matrix products, arithmetic and copies ran while one was open for 27% of the time, Pallas kernels for 0%

commit v1 on v0

v1 whole, which is shorter than its diff:
```python
import jax
import jax.numpy as jnp
from jax import lax
from jax.experimental import pallas as pl
from jax.experimental.pallas import tpu as pltpu
from jax.sharding import PartitionSpec as P

HD = 128
GROUP = 8
KV_HEADS = 4
ROWS = 96
BLOCK = 48
KEYS = 1536
SHORT = 64
TILE = 256
TILES = KEYS // TILE
N_DP = 16
SCALE = HD**-0.5
LOG2E = 1.4426950408889634
NT = (((1,), (1,)), ((), ()))
F32 = jnp.float32
BF16 = jnp.bfloat16
MESH = pl.DeviceIdType.MESH


def dot(a, b):
    return jnp.dot(a, b, preferred_element_type=F32)


def dot_nt(a, b):
    return lax.dot_general(a, b, NT, preferred_element_type=F32)


def kernel(
    lq, lk, lv, lc, bo, sq, sk, sv, sc, dl, bl,
    lo, ldq, ldk, ldv, so, sdq, sdk, sdv,
    kv, kvx, qb, cb, qh, ch, oh, dqh, ob, dqb, kmat, vmat, ktr, vtr, qps, sbuf, pbuf, acc,
    rs_s, rs_r, rz_o, rz_s, rz_r, rfin,
    st, r1, s2, r2, qs, cs, ks, vs,
    ag_send, ag_recv, qx_send, qx_recv, loc, p1_send, p1_recv, p2_send, p2_recv,
    ry_send, ry_recv, rz_send, rz_recv, fin_send, fin_recv, out_send, out_recv,
):
    d = lax.axis_index("dp")
    c = lax.axis_index("ctx")
    h = c % 2
    y = (c // 2) % 4
    zh = c // 8
    sib = {"ctx": c + 1 - 2 * h}
    anti = {"ctx": (c + 8) % 16}

    def at_y(k):
        return {"ctx": zh * 8 + ((y + k) % 4) * 2 + h}

    def at_dp(k):
        return {"dp": (d + k) % N_DP}

    def remote(src, dst, send, recv, to):
        return pltpu.make_async_remote_copy(
            src_ref=src, dst_ref=dst, send_sem=send, recv_sem=recv, device_id=to, device_id_type=MESH
        )

    barrier = pltpu.get_barrier_semaphore()
    peers = [sib, anti] + [at_y(k) for k in range(1, 4)] + [at_dp(k) for k in range(1, N_DP)]
    for peer in peers:
        pl.semaphore_signal(barrier, inc=1, device_id=peer, device_id_type=MESH)

    mine = pl.ds(pl.multiple_of(h * 256, 256), 256)
    other = pl.ds(pl.multiple_of((1 - h) * 256, 256), 256)
    kv[zh, y, h, 0] = lk[0, :, mine]
    kv[zh, y, h, 1] = lv[0, :, mine]
    kvx[0] = lk[0, :, other]
    kvx[1] = lv[0, :, other]
    for a in range(4):
        for b in range(4):
            rows = slice(16 * a, 16 * a + 16)
            st[4 * a + b, :, 0:1024] = sq[0, rows, 1024 * b : 1024 * b + 1024]
            st[4 * a + b, :, 1024:1152] = sk[0, rows, 128 * b : 128 * b + 128]
            st[4 * a + b, :, 1152:1280] = sv[0, rows, 128 * b : 128 * b + 128]
    r1[0] = st[0]
    for part in range(3):
        column = lax.broadcasted_iota(jnp.int32, (1, TILE), 1) + part * TILE
        position = jnp.zeros((1, TILE), jnp.int32)
        for k in range(16):
            start = bo[0, zh * 16 + y * 4 + k % 4] * BLOCK - BLOCK * k
            position = jnp.where(column >= BLOCK * k, column + start, position)
        qps[part] = position

    pl.semaphore_wait(barrier, len(peers))

    waits = []

    def begin(copy):
        copy.start()
        waits.append(copy)
        return copy

    sib_kv = begin(remote(kvx, kv.at[zh, y, h], ag_send.at[0], ag_recv.at[0], sib))
    wide_mine = pl.ds(pl.multiple_of(h * 2048, 2048), 2048)
    wide_other = pl.ds(pl.multiple_of((1 - h) * 2048, 2048), 2048)
    sib_q = begin(remote(lq.at[0, :, wide_other], qb.at[h], qx_send.at[0], qx_recv.at[0], sib))
    sib_c = begin(remote(lc.at[0, :, wide_other], cb.at[h], qx_send.at[1], qx_recv.at[1], sib))
    own_q = pltpu.make_async_copy(lq.at[0, :, wide_mine], qb.at[h], loc.at[0])
    own_c = pltpu.make_async_copy(lc.at[0, :, wide_mine], cb.at[h], loc.at[1])
    own_q.start()
    own_c.start()
    sib_kv.wait_recv()
    zcopy = begin(remote(kv.at[zh, y], kv.at[zh, y], ag_send.at[1], ag_recv.at[1], anti))
    up = begin(remote(kv.at[zh, y], kv.at[zh, y], ag_send.at[2], ag_recv.at[2], at_y(1)))
    down = begin(remote(kv.at[zh, y], kv.at[zh, y], ag_send.at[3], ag_recv.at[3], at_y(3)))
    first = [
        begin(remote(st.at[p], r1.at[p], p1_send.at[p], p1_recv.at[p], at_dp(p)))
        for p in range(1, N_DP)
    ]
    own_q.wait()
    own_c.wait()
    sib_q.wait_recv()
    sib_c.wait_recv()
    for g in range(2):
        for j in range(GROUP):
            for r in range(2):
                to = slice(j * 192 + r * ROWS, j * 192 + r * ROWS + ROWS)
                at = slice((g * GROUP + j) * HD, (g * GROUP + j + 1) * HD)
                qh[g, to, :] = qb[r, :, at]
                ch[g, to, :] = cb[r, :, at]
    ylow, yhigh = (y + 3) % 4, (y + 1) % 4
    up.wait_recv()
    relay0 = begin(
        remote(kv.at[zh, ylow, 0], kv.at[zh, ylow, 0], ag_send.at[4], ag_recv.at[4], at_y(1))
    )
    down.wait_recv()
    relay1 = begin(
        remote(kv.at[zh, yhigh, 1], kv.at[zh, yhigh, 1], ag_send.at[5], ag_recv.at[5], at_y(3))
    )
    zcopy.wait_recv()
    zo = 1 - zh
    up2 = begin(remote(kv.at[zo, y], kv.at[zo, y], ag_send.at[6], ag_recv.at[6], at_y(1)))
    down2 = begin(remote(kv.at[zo, y], kv.at[zo, y], ag_send.at[7], ag_recv.at[7], at_y(3)))
    up2.wait_recv()
    relay2 = begin(
        remote(kv.at[zo, ylow, 0], kv.at[zo, ylow, 0], ag_send.at[8], ag_recv.at[8], at_y(1))
    )
    down2.wait_recv()
    relay3 = begin(
        remote(kv.at[zo, yhigh, 1], kv.at[zo, yhigh, 1], ag_send.at[9], ag_recv.at[9], at_y(3))
    )
    for copy in (relay0, relay1, relay2, relay3):
        copy.wait_recv()

    sub = lax.broadcasted_iota(jnp.int32, (BLOCK, TILE), 0)

    def attend(g):
        kmat[...] = kv[:, :, :, 0, :, g * HD : (g + 1) * HD].reshape(KEYS, HD)
        vmat[...] = kv[:, :, :, 1, :, g * HD : (g + 1) * HD].reshape(KEYS, HD)
        ktr[...] = kmat[...].T
        vtr[...] = vmat[...].T
        acc[...] = jnp.zeros_like(acc)

        def tile(t, carry):
            rows = pl.ds(pl.multiple_of(t * TILE, TILE), TILE)
            qt = qh[g, rows, :]
            ct = ch[g, rows, :]
            qp = qps[t % 3]
            s = dot_nt(kmat[...], qt)
            top = jnp.full((8, TILE), -1e30, F32)
            for b in range(KEYS // BLOCK):
                at = slice(b * BLOCK, (b + 1) * BLOCK)
                block = jnp.where(sub <= qp - bo[0, b] * BLOCK, s[at] * (SCALE * LOG2E), -1e30)
                sbuf[at, :] = block
                top = jnp.maximum(top, jnp.max(block.reshape(6, 8, TILE), axis=0))
            top = jnp.max(top, axis=0, keepdims=True)
            total = jnp.zeros((8, TILE), F32)
            for b in range(KEYS // BLOCK):
                at = slice(b * BLOCK, (b + 1) * BLOCK)
                block = jnp.exp2(sbuf[at, :] - top)
                sbuf[at, :] = block
                total = total + jnp.sum(block.reshape(6, 8, TILE), axis=0)
            inverse = 1.0 / jnp.sum(total, axis=0, keepdims=True)
            for b in range(KEYS // BLOCK):
                at = slice(b * BLOCK, (b + 1) * BLOCK)
                pbuf[at, :] = (sbuf[at, :] * inverse).astype(BF16)
            out = dot(vtr[...], pbuf[...])
            acc[:, HD:] += dot(pbuf[...], ct)
            oh[g, rows, :] = out.T.astype(BF16)
            delta = jnp.sum(out.astype(BF16).astype(F32) * ct.astype(F32).T, axis=0, keepdims=True)
            dprobs = dot_nt(vmat[...], ct)
            for b in range(KEYS // BLOCK):
                at = slice(b * BLOCK, (b + 1) * BLOCK)
                pbuf[at, :] = (sbuf[at, :] * ((dprobs[at] - delta) * inverse)).astype(BF16)
            dq = dot(ktr[...], pbuf[...])
            acc[:, :HD] += dot(pbuf[...], qt)
            dqh[g, rows, :] = (dq * SCALE).T.astype(BF16)
            return carry

        lax.fori_loop(0, TILES, tile, 0)

    def give(g):
        for z in range(2):
            for row in range(4):
                part = acc[(z * 4 + row) * 192 : (z * 4 + row + 1) * 192, :]
                rs_s[g, row, z, :, :, :HD] = (part[:, :HD] * SCALE).astype(BF16).reshape(2, ROWS, HD)
                rs_s[g, row, z, :, :, HD:] = part[:, HD:].astype(BF16).reshape(2, ROWS, HD)
        copies = [
            begin(
                remote(
                    rs_s.at[g, (y + k) % 4],
                    rs_r.at[g, k - 1],
                    ry_send.at[3 * g + k - 1],
                    ry_recv.at[3 * g + k - 1],
                    at_y(k),
                )
            )
            for k in range(1, 4)
        ]
        for j in range(GROUP):
            for r in range(2):
                at = slice(j * 192 + r * ROWS, j * 192 + r * ROWS + ROWS)
                ob[g, r, :, j * HD : (j + 1) * HD] = oh[g, at, :]
                dqb[g, r, :, j * HD : (j + 1) * HD] = dqh[g, at, :]
        place = pl.ds(pl.multiple_of(h * 2048 + g * 1024, 1024), 1024)
        outs = []
        for i, (source, target) in enumerate(((ob, lo), (dqb, ldq))):
            begin_at = 2 * g + i
            outs.append(
                begin(
                    remote(
                        source.at[g, 1 - h],
                        target.at[0, :, place],
                        out_send.at[begin_at],
                        out_recv.at[begin_at],
                        sib,
                    )
                )
            )
            own = pltpu.make_async_copy(
                source.at[g, h], target.at[0, :, place], loc.at[2 + begin_at]
            )
            own.start()
            outs.append(own)
        return copies, outs

    attend(0)
    mask = bl[0, 0]
    for copy in first:
        copy.wait_recv()
    for k in range(N_DP):
        s2[k] = r1[(d - ((d + k) % N_DP ^ mask) + N_DP) % N_DP]
    r2[0] = s2[0]
    second = [
        begin(remote(s2.at[k], r2.at[k], p2_send.at[k], p2_recv.at[k], at_dp(k)))
        for k in range(1, N_DP)
    ]
    copies0, outs0 = give(0)
    attend(1)
    copies1, outs1 = give(1)

    def reduce_y(g, copies):
        for copy in copies:
            copy.wait_recv()
        def total(z):
            value = rs_s[g, y, z].astype(F32)
            for k in range(3):
                value = value + rs_r[g, k, z].astype(F32)
            return value
        rz_s[g] = total(1 - zh).astype(BF16)
        sent = begin(remote(rz_s.at[g], rz_r.at[g], rz_send.at[g], rz_recv.at[g], anti))
        rz_o[g] = total(zh)
        return sent

    def reduce_z(g, sent):
        sent.wait_recv()
        rfin[g] = (rz_o[g] + rz_r[g].astype(F32)).astype(BF16)
        place = pl.ds(pl.multiple_of(h * 256 + g * HD, HD), HD)
        finals = []
        for i, target in enumerate((ldk, ldv)):
            at = 2 * g + i
            lanes = pl.ds(i * HD, HD)
            finals.append(
                begin(
                    remote(
                        rfin.at[g, 1 - h, :, lanes],
                        target.at[0, :, place],
                        fin_send.at[at],
                        fin_recv.at[at],
                        sib,
                    )
                )
            )
            own = pltpu.make_async_copy(
                rfin.at[g, h, :, lanes], target.at[0, :, place], loc.at[6 + at]
            )
            own.start()
            finals.append(own)
        return finals

    z0 = reduce_y(0, copies0)
    for copy in second:
        copy.wait_recv()
    z1 = reduce_y(1, copies1)

    source = d ^ mask
    base = d - source + 2 * N_DP
    for a in range(4):
        for b in range(4):
            piece = r2[(base - (4 * a + b)) % N_DP]
            ks[b, 16 * a : 16 * a + 16, :] = piece[:, 1024:1152]
            vs[b, 16 * a : 16 * a + 16, :] = piece[:, 1152:1280]
            for j in range(GROUP):
                qs[b, j * SHORT + 16 * a : j * SHORT + 16 * a + 16, :] = piece[
                    :, j * HD : (j + 1) * HD
                ]
    width = GROUP * SHORT
    for b in range(4):
        for j in range(GROUP):
            at = (b * GROUP + j) * HD
            cs[b, j * SHORT : (j + 1) * SHORT, :] = sc[0, :, at : at + HD]
    key_row = lax.broadcasted_iota(jnp.int32, (SHORT, width), 0)
    query_row = lax.broadcasted_iota(jnp.int32, (SHORT, width), 1) & (SHORT - 1)
    key_doc = jnp.zeros((SHORT, width), jnp.int32)
    query_doc = jnp.zeros((SHORT, width), jnp.int32)
    end = jnp.int32(0)
    for k in range(4):
        end = end + dl[source, 0, k]
        key_doc = key_doc + jnp.where(key_row >= end, 1, 0)
        query_doc = query_doc + jnp.where(query_row >= end, 1, 0)
    allowed = (key_doc == query_doc) & (key_row <= query_row)
    for b in range(KV_HEADS):
        qt, ct, kt, vt = qs[b], cs[b], ks[b], vs[b]
        s = jnp.where(allowed, dot_nt(kt, qt) * (SCALE * LOG2E), -1e30)
        s = jnp.exp2(s - jnp.max(s, axis=0, keepdims=True))
        probs = s * (1.0 / jnp.sum(s, axis=0, keepdims=True))
        low = probs.astype(BF16)
        out = dot(vt.astype(F32).T.astype(BF16), low)
        sdv[0, :, b * HD : (b + 1) * HD] = dot(low, ct).astype(BF16)
        delta = jnp.sum(out.astype(BF16).astype(F32) * ct.astype(F32).T, axis=0, keepdims=True)
        ds = (probs * (dot_nt(vt, ct) - delta)).astype(BF16)
        dq = dot(kt.astype(F32).T.astype(BF16), ds) * SCALE
        sdk[0, :, b * HD : (b + 1) * HD] = (dot(ds, qt) * SCALE).astype(BF16)
        out = out.T.astype(BF16)
        dq = dq.T.astype(BF16)
        for j in range(GROUP):
            at = (b * GROUP + j) * HD
            so[0, :, at : at + HD] = out[j * SHORT : (j + 1) * SHORT]
            sdq[0, :, at : at + HD] = dq[j * SHORT : (j + 1) * SHORT]

    finals = reduce_z(0, z0) + reduce_z(1, z1)
    for copy in outs0[1::2] + outs1[1::2] + finals[1::2]:
        copy.wait()
    for copy in outs0[0::2] + outs1[0::2] + finals[0::2]:
        copy.wait_recv()
    for copy in waits:
        copy.wait_send()


def per_device(*args):
    any_spec = pl.BlockSpec(memory_space=pl.ANY)
    vmem = pl.BlockSpec(memory_space=pltpu.VMEM)
    smem = pl.BlockSpec(memory_space=pltpu.SMEM)
    dma = pltpu.SemaphoreType.DMA
    long_query, long_key, short_query, short_key = args[0], args[1], args[5], args[6]

    def shape(like):
        return jax.ShapeDtypeStruct(like.shape, like.dtype)

    def buffer(*dims, dtype=BF16):
        return pltpu.VMEM(dims, dtype)

    return pl.pallas_call(
        kernel,
        out_shape=(
            shape(long_query), shape(long_query), shape(long_key), shape(long_key),
            shape(short_query), shape(short_query), shape(short_key), shape(short_key),
        ),
        in_specs=[any_spec, vmem, vmem, any_spec, smem, vmem, vmem, vmem, vmem, smem, smem],
        out_specs=(any_spec,) * 4 + (vmem,) * 4,
        scratch_shapes=[
            buffer(2, 4, 2, 2, ROWS, 256),
            buffer(2, ROWS, 256),
            buffer(2, ROWS, 2048),
            buffer(2, ROWS, 2048),
            buffer(2, KEYS, HD),
            buffer(2, KEYS, HD),
            buffer(2, KEYS, HD),
            buffer(2, KEYS, HD),
            buffer(2, 2, ROWS, 1024),
            buffer(2, 2, ROWS, 1024),
            buffer(KEYS, HD),
            buffer(KEYS, HD),
            buffer(HD, KEYS),
            buffer(HD, KEYS),
            buffer(3, 1, TILE, dtype=jnp.int32),
            buffer(KEYS, TILE, dtype=F32),
            buffer(KEYS, TILE),
            buffer(KEYS, 256, dtype=F32),
            buffer(2, 4, 2, 2, ROWS, 256),
            buffer(2, 3, 2, 2, ROWS, 256),
            buffer(2, 2, ROWS, 256, dtype=F32),
            buffer(2, 2, ROWS, 256),
            buffer(2, 2, ROWS, 256),
            buffer(2, 2, ROWS, 256),
            buffer(N_DP, 16, 1280),
            buffer(N_DP, 16, 1280),
            buffer(N_DP, 16, 1280),
            buffer(N_DP, 16, 1280),
            buffer(4, GROUP * SHORT, HD),
            buffer(4, GROUP * SHORT, HD),
            buffer(4, SHORT, HD),
            buffer(4, SHORT, HD),
            dma((10,)), dma((10,)), dma((2,)), dma((2,)), dma((10,)),
            dma((N_DP,)), dma((N_DP,)), dma((N_DP,)), dma((N_DP,)),
            dma((6,)), dma((6,)), dma((2,)), dma((2,)), dma((4,)), dma((4,)), dma((4,)), dma((4,)),
        ],
        compiler_params=pltpu.CompilerParams(
            collective_id=0, has_side_effects=True, vmem_limit_bytes=48 * 1024 * 1024
        ),
    )(*args)


def solution(mesh):
    wide = P("dp", "ctx", None)
    return jax.shard_map(
        per_device,
        mesh=mesh,
        in_specs=(wide,) * 4
        + (P("dp", None),)
        + (wide,) * 4
        + (P(None, "ctx", None), P("ctx", None)),
        out_specs=(wide,) * 8,
        check_vma=False,
    )
```

time: 545 us -> 97.4 us (0.18)
  waiting for transfers between devices: 355 us -> 0 us
  matrix products: 91.8 us -> 0 us
  Pallas kernels: 0 us -> 80.6 us
  other arithmetic: 43.3 us -> 0 us
  local copies, waits for them, and re-layouts: 32.3 us -> 14.5 us
  between operations: 17.3 us -> 0.67 us
    all_gather x5 -> x0, waiting for transfers between devices: 237 us -> none  [the longest x1 99.6 us: per_device(): lax.all_gather(short_query[0], 'dp', axis=0, tiled=True)]
    reduce_scatter x1 -> x0, waiting for transfers between devices: 115 us -> none  [per_device(): lax.psum_scatter(jnp.concatenate([key_block, value_block], axis=1), 'ctx'...]
    pallas_call x0 -> x1, Pallas kernels: none -> 80.6 us  [per_device(): pl.pallas_call(kernel, out_shape=(shape(long_query), shape(long_query), s...]
    dot_general x43 -> x0, matrix products: 73.5 us -> none  [the longest x8 26.2 us: key_value_grads(): jnp.einsum('grk,rgd->kd', probs_low, cotangent, preferred_element_type=jn...]
    reduce_sum x14 -> x0, other arithmetic: 30.6 us -> none  [the longest x8 28.8 us: attend(): total = jnp.sum(jnp.exp(masked - highest), axis=2, keepdims=True)]
    sub x8 -> x0, matrix products: 18.4 us -> none  [attend(): probs = jnp.exp(masked - highest - jnp.log(total))]
    reshape x4 -> x0, local copies, waits for them, and re-layouts: 7.72 us -> none  [the longest x1 2.39 us: per_device(): jnp.stack(key_parts, axis=1)]
    unnamed x100 -> x29, local copies, waits for them, and re-layouts: 7.17 us -> 14.5 us
  transfers between devices with their start and end apart: 6 -> 0, of which waited for: 5 -> 0; matrix products, arithmetic and copies ran while one was open for 27% -> 0% of each run, Pallas kernels for 0% -> 0%
where the time goes in v1:
time: 97.4 us; the launch traced here: 95.7 us
  Pallas kernels  80.6 us (83%)
  local copies, waits for them, and re-layouts  14.5 us (15%)
    pallas_call x1, Pallas kernels, per_device(): pl.pallas_call(kernel, out_shape=(shape(long_query), shape(long_query), s...  80.6 us
    unnamed x29, local copies, waits for them, and re-layouts  14.5 us

profile of v1, /device:TPU:1, one launch (start us, length us, event | category | flops | bytes accessed | tf_op | source)
XLA Modules:
  0.0 95.7 jit_solution(15525508140640270683)
XLA Ops:
  0.6 0.0 copy-start.9
  0.6 0.0 copy-start.8
  0.7 0.8 copy.19.dl
  1.4 0.0 copy-done.9
  1.4 0.0 copy-done.8
  1.4 0.0 copy-start
  1.4 1.1 %copy-done = bf16[1,96,4096]{2,1,0:T(8,128)(2,1)S(1)} copy-done((bf16[1,96,4096]{2,1,0:T(8,128)(2,1)S(1)}, bf16[1,96,4096]{2,1,0:T(8,128)(2,1)}, u32[]{:S(2)}) %copy-start) | copy-done | bytes 786456
  2.6 0.0 copy-start.1
  2.6 1.1 %copy-done.1 = bf16[1,96,4096]{2,1,0:T(8,128)(2,1)S(1)} copy-done((bf16[1,96,4096]{2,1,0:T(8,128)(2,1)S(1)}, bf16[1,96,4096]{2,1,0:T(8,128)(2,1)}, u32[]{:S(2)}) %copy-start.1) | copy-done | bytes 786456
  3.7 1.0 %copy-done.2 = bf16[1,64,4096]{2,1,0:T(8,128)(2,1)S(1)} copy-done((bf16[1,64,4096]{2,1,0:T(8,128)(2,1)S(1)}, bf16[1,64,4096]{2,1,0:T(8,128)(2,1)}, u32[]{:S(2)}) %copy-start.2) | copy-done | bytes 524312
  4.7 1.0 %copy-done.3 = bf16[1,64,4096]{2,1,0:T(8,128)(2,1)S(1)} copy-done((bf16[1,64,4096]{2,1,0:T(8,128)(2,1)S(1)}, bf16[1,64,4096]{2,1,0:T(8,128)(2,1)}, u32[]{:S(2)}) %copy-start.3) | copy-done | bytes 524312
  5.8 0.9 copy-done.4
  6.7 0.9 copy-done.5
  7.6 0.8 copy-done.6
  8.4 0.8 copy-done.7
  9.2 80.6 %shard_map.170 = (bf16[1,96,4096]{2,1,0:T(8,128)(2,1)S(1)}, bf16[1,96,4096]{2,1,0:T(8,128)(2,1)S(1)}, bf16[1,96,512]{2,1,0:T(8,128)(2,1)S(1)}, bf16[1,96,512]{2,...) custom-call(bf16[1,96,4096]{2,1,0:T(8,128)(2,1)S(1)} %copy-done, ...), custom_call_target="tpu_custom_call" | custom-call | tf_op jit(solution)/shard_map/pallas_call | solution.py:367
  89.8 0.9 copy.28
  90.7 0.9 copy.29
  91.6 0.6 copy.30
  92.2 0.6 copy.31
  92.9 0.8 copy.32
  93.7 0.8 copy.33
  94.5 0.6 copy.34
  95.1 0.6 copy.35
  (6 shorter events, 0.0 us)
Async XLA Ops:
  0.6 0.8 copy-start.9
  0.6 0.8 copy-start.8
  1.4 1.1 %copy-start = (bf16[1,96,4096]{2,1,0:T(8,128)(2,1)S(1)}, bf16[1,96,4096]{2,1,0:T(8,128)(2,1)}, u32[]{:S(2)}) copy-start(bf16[1,96,4096]{2,1,0:T(8,128)(2,1)} %lq.1) | copy-start | bytes 2359300
  2.6 1.1 %copy-start.1 = (bf16[1,96,4096]{2,1,0:T(8,128)(2,1)S(1)}, bf16[1,96,4096]{2,1,0:T(8,128)(2,1)}, u32[]{:S(2)}) copy-start(bf16[1,96,4096]{2,1,0:T(8,128)(2,1)} %lc.1) | copy-start | bytes 2359300
  3.7 1.0 %copy-start.2 = (bf16[1,64,4096]{2,1,0:T(8,128)(2,1)S(1)}, bf16[1,64,4096]{2,1,0:T(8,128)(2,1)}, u32[]{:S(2)}) copy-start(bf16[1,64,4096]{2,1,0:T(8,128)(2,1)} %sq.1) | copy-start | bytes 1572868
  4.7 1.0 %copy-start.3 = (bf16[1,64,4096]{2,1,0:T(8,128)(2,1)S(1)}, bf16[1,64,4096]{2,1,0:T(8,128)(2,1)}, u32[]{:S(2)}) copy-start(bf16[1,64,4096]{2,1,0:T(8,128)(2,1)} %sc.1) | copy-start | bytes 1572868
  5.8 0.9 copy-start.4
  6.7 0.9 copy-start.5
  7.6 0.8 copy-start.6
  8.4 0.8 copy-start.7

commit v2 on v1

v2 whole, which is shorter than its diff:
```python
import jax
import jax.numpy as jnp
from jax import lax
from jax.experimental import pallas as pl
from jax.experimental.pallas import tpu as pltpu
from jax.sharding import PartitionSpec as P

HD = 128
GROUP = 8
KV_HEADS = 4
ROWS = 96
BLOCK = 48
KEYS = 1536
SHORT = 64
TILE = 256
TILES = KEYS // TILE
N_DP = 16
SEMS = 96
VMEM_LIMIT = 62 * 1024 * 1024
FIRST_EARLY = True
FAR_AT = 1
SECOND_AT = 5
SUM_AT = 10
SCALE = HD**-0.5
LOG2E = 1.4426950408889634
NT = (((1,), (1,)), ((), ()))
F32 = jnp.float32
BF16 = jnp.bfloat16
MESH = pl.DeviceIdType.MESH


def dot(a, b):
    return jnp.dot(a, b, preferred_element_type=F32)


def dot_nt(a, b):
    return lax.dot_general(a, b, NT, preferred_element_type=F32)


def kernel(
    lq, lk, lv, lc, bo, sq, sk, sv, sc, dl, bl,
    lo, ldq, ldk, ldv, so, sdq, sdk, sdv,
    lkb, lvb, sqb, skb, svb, scb,
    kv, kvx, qb, cb, qh, ch, oh, dqh, ob, dqb, kmat, vmat, ktr, vtr, qps, sbuf, pbuf, acc,
    rs_s, rs_r, rz_o, rz_s, rz_r, rfin,
    st, r1, s2, r2, qs, cs, ks, vs,
    loc, sends, recvs,
):
    d = lax.axis_index("dp")
    c = lax.axis_index("ctx")
    h = c % 2
    y = (c // 2) % 4
    zh = c // 8
    zo = 1 - zh
    ylow, yhigh = (y + 3) % 4, (y + 1) % 4
    sib = {"ctx": c + 1 - 2 * h}
    anti = {"ctx": (c + 8) % 16}
    mask = bl[0, 0]

    def at_y(k):
        return {"ctx": zh * 8 + ((y + k) % 4) * 2 + h}

    def at_dp(k):
        return {"dp": (d + k) % N_DP}

    numbers = {}

    def remote(name, src, dst, to):
        number = numbers.setdefault(name, len(numbers))
        return pltpu.make_async_remote_copy(
            src_ref=src,
            dst_ref=dst,
            send_sem=sends.at[number],
            recv_sem=recvs.at[number],
            device_id=to,
            device_id_type=MESH,
        )

    barrier = pltpu.get_barrier_semaphore()
    peers = [sib, anti] + [at_y(k) for k in range(1, 4)] + [at_dp(k) for k in range(1, N_DP)]
    for peer in peers:
        pl.semaphore_signal(barrier, inc=1, device_id=peer, device_id_type=MESH)

    local = []

    def load(src, dst):
        copy = pltpu.make_async_copy(src, dst, loc.at[len(local)])
        copy.start()
        local.append(copy)
        return copy

    load_k, load_v = load(lk.at[0], lkb), load(lv.at[0], lvb)
    load_s = [load(sq.at[0], sqb), load(sk.at[0], skb), load(sv.at[0], svb)]

    def wide(core, g):
        return pl.ds(pl.multiple_of(core * 2048 + g * 1024, 1024), 1024)

    own_rows = [
        [load(lq.at[0, :, wide(h, g)], qb.at[g, h]), load(lc.at[0, :, wide(h, g)], cb.at[g, h])]
        for g in range(2)
    ]
    load_c = load(sc.at[0], scb)

    for part in range(3):
        column = lax.broadcasted_iota(jnp.int32, (1, TILE), 1) + part * TILE
        position = jnp.zeros((1, TILE), jnp.int32)
        for k in range(16):
            start = bo[0, zh * 16 + y * 4 + k % 4] * BLOCK - BLOCK * k
            position = jnp.where(column >= BLOCK * k, column + start, position)
        qps[part] = position

    load_k.wait()
    load_v.wait()
    for g in range(2):
        mine = pl.ds(pl.multiple_of(h * 256 + g * HD, HD), HD)
        other = pl.ds(pl.multiple_of((1 - h) * 256 + g * HD, HD), HD)
        kv[g, zh, y, h, 0] = lkb[:, mine]
        kv[g, zh, y, h, 1] = lvb[:, mine]
        kvx[g, 0] = lkb[:, other]
        kvx[g, 1] = lvb[:, other]

    pl.semaphore_wait(barrier, len(peers))

    waits = []

    def begin(copy):
        copy.start()
        waits.append(copy)
        return copy

    def same(name, block, to):
        return remote(name, block, block, to)

    sib_kv = [
        begin(remote(f"sib{g}", kvx.at[g], kv.at[g, zh, y, h], sib)) for g in range(2)
    ]
    zc, own_y = [], []
    for g in range(2):
        mine = begin(same(f"z{g}own", kv.at[g, zh, y, h], anti))
        sib_kv[g].wait_recv()
        zc.append([mine, begin(same(f"z{g}sib", kv.at[g, zh, y, 1 - h], anti))])
        own_y.append(
            [
                begin(same(f"up{g}", kv.at[g, zh, y], at_y(1))),
                begin(same(f"down{g}", kv.at[g, zh, y], at_y(3))),
            ]
        )
        if g == 0:
            sib_rows = [
                [
                    begin(remote(f"q{k}", lq.at[0, :, wide(1 - h, k)], qb.at[k, h], sib)),
                    begin(remote(f"c{k}", lc.at[0, :, wide(1 - h, k)], cb.at[k, h], sib)),
                ]
                for k in range(2)
            ]

    def first():
        return [remote(f"first{p}", st.at[p], r1.at[p], at_dp(p)) for p in range(1, N_DP)]

    def second():
        return [remote(f"second{p}", s2.at[p], r2.at[p], at_dp(p)) for p in range(1, N_DP)]

    def begin_first():
        for copy in load_s:
            copy.wait()
        for a in range(4):
            for b in range(4):
                rows = slice(16 * a, 16 * a + 16)
                st[4 * a + b, :, 0:1024] = sqb[rows, 1024 * b : 1024 * b + 1024]
                st[4 * a + b, :, 1024:1152] = skb[rows, 128 * b : 128 * b + 128]
                st[4 * a + b, :, 1152:1280] = svb[rows, 128 * b : 128 * b + 128]
        r1[0] = st[0]
        for copy in first():
            copy.start()

    def begin_second():
        for copy in first():
            copy.wait_recv()
        for k in range(N_DP):
            s2[k] = r1[(d - ((d + k) % N_DP ^ mask) + N_DP) % N_DP]
        r2[0] = s2[0]
        for copy in second():
            copy.start()

    if FIRST_EARLY:
        begin_first()

    def arrange(g):
        for copy in own_rows[g]:
            copy.wait()
        for copy in sib_rows[g]:
            copy.wait_recv()
        for j in range(GROUP):
            for r in range(2):
                to = slice(j * 192 + r * ROWS, j * 192 + r * ROWS + ROWS)
                at = slice(j * HD, (j + 1) * HD)
                qh[g, to, :] = qb[g, r, :, at]
                ch[g, to, :] = cb[g, r, :, at]

    def relays(g, z, name):
        return [
            same(f"relay{g}{name}0", kv.at[g, z, ylow, 0], at_y(1)),
            same(f"relay{g}{name}1", kv.at[g, z, yhigh, 1], at_y(3)),
        ]

    def far_y(g):
        return [
            same(f"upfar{g}", kv.at[g, zo, y], at_y(1)),
            same(f"downfar{g}", kv.at[g, zo, y], at_y(3)),
        ]

    def pass_on(arrived, onward):
        for copy, after in zip(arrived, onward):
            copy.wait_recv()
            after.start()

    arrange(0)
    pass_on(own_y[0], relays(0, zh, "n"))
    for copy in zc[0]:
        copy.wait_recv()
    for copy in far_y(0):
        copy.start()
    pass_on(own_y[1], relays(1, zh, "n"))
    arrange(1)
    pass_on(far_y(0), relays(0, zo, "f"))
    for copy in zc[1]:
        copy.wait_recv()
    for copy in far_y(1):
        copy.start()
    if not FIRST_EARLY:
        begin_first()

    sub = lax.broadcasted_iota(jnp.int32, (BLOCK, TILE), 0)

    def heads(g):
        for copy in relays(g, zh, "n") + relays(g, zo, "f"):
            copy.wait_recv()
        kmat[...] = kv[g, :, :, :, 0].reshape(KEYS, HD)
        vmat[...] = kv[g, :, :, :, 1].reshape(KEYS, HD)
        ktr[...] = kmat[...].T
        vtr[...] = vmat[...].T
        acc[...] = jnp.zeros_like(acc)

    def sums_y(g):
        return [
            remote(f"sum{g}{k}", rs_s.at[g, (y + k) % 4], rs_r.at[g, k - 1], at_y(k))
            for k in (2, 1, 3)
        ]

    def results(g):
        copies, own = [], []
        for i, (source, target) in enumerate(((ob, lo), (dqb, ldq))):
            place = target.at[0, :, wide(h, g)]
            copies.append(remote(f"out{g}{i}", source.at[g, 1 - h], place, sib))
            own.append(pltpu.make_async_copy(source.at[g, h], place, loc.at[16 + 2 * g + i]))
        return copies, own

    def give(g):
        for z in range(2):
            for row in range(4):
                part = acc[(z * 4 + row) * 192 : (z * 4 + row + 1) * 192, :]
                rs_s[g, row, z, :, :, :HD] = (
                    (part[:, :HD] * SCALE).astype(BF16).reshape(2, ROWS, HD)
                )
                rs_s[g, row, z, :, :, HD:] = part[:, HD:].astype(BF16).reshape(2, ROWS, HD)
        for copy in sums_y(g):
            copy.start()
        for j in range(GROUP):
            for r in range(2):
                at = slice(j * 192 + r * ROWS, j * 192 + r * ROWS + ROWS)
                ob[g, r, :, j * HD : (j + 1) * HD] = oh[g, at, :]
                dqb[g, r, :, j * HD : (j + 1) * HD] = dqh[g, at, :]
        copies, own = results(g)
        for copy in copies + own:
            copy.start()

    def sum_z(g):
        return remote(f"sumz{g}", rz_s.at[g], rz_r.at[g], anti)

    def reduce_y(g):
        for copy in sums_y(g):
            copy.wait_recv()

        def total(z):
            value = rs_s[g, y, z].astype(F32)
            for k in range(3):
                value = value + rs_r[g, k, z].astype(F32)
            return value

        rz_s[g] = total(zo).astype(BF16)
        sum_z(g).start()
        rz_o[g] = total(zh)

    def finals(g):
        copies, own = [], []
        place = pl.ds(pl.multiple_of(h * 256 + g * HD, HD), HD)
        for i, target in enumerate((ldk, ldv)):
            lanes = pl.ds(i * HD, HD)
            to = target.at[0, :, place]
            copies.append(remote(f"final{g}{i}", rfin.at[g, 1 - h, :, lanes], to, sib))
            own.append(
                pltpu.make_async_copy(rfin.at[g, h, :, lanes], to, loc.at[20 + 2 * g + i])
            )
        return copies, own

    def reduce_z(g):
        sum_z(g).wait_recv()
        rfin[g] = (rz_o[g] + rz_r[g].astype(F32)).astype(BF16)
        copies, own = finals(g)
        for copy in copies + own:
            copy.start()

    def tile(i, carry):
        g, t = i // TILES, i % TILES

        @pl.when(i == 0)
        def _():
            heads(0)

        @pl.when(i == FAR_AT)
        def _():
            pass_on(far_y(1), relays(1, zo, "f"))

        @pl.when(i == SECOND_AT)
        def _():
            begin_second()

        @pl.when(i == TILES)
        def _():
            give(0)
            heads(1)

        @pl.when(i == SUM_AT)
        def _():
            reduce_y(0)

        rows = pl.ds(pl.multiple_of(t * TILE, TILE), TILE)
        qt = qh[g, rows, :]
        ct = ch[g, rows, :]
        qp = qps[t % 3]
        s = dot_nt(kmat[...], qt)
        top = jnp.full((8, TILE), -1e30, F32)
        for b in range(KEYS // BLOCK):
            at = slice(b * BLOCK, (b + 1) * BLOCK)
            block = jnp.where(sub <= qp - bo[0, b] * BLOCK, s[at] * (SCALE * LOG2E), -1e30)
            sbuf[at, :] = block
            top = jnp.maximum(top, jnp.max(block.reshape(6, 8, TILE), axis=0))
        top = jnp.max(top, axis=0, keepdims=True)
        total = jnp.zeros((8, TILE), F32)
        for b in range(KEYS // BLOCK):
            at = slice(b * BLOCK, (b + 1) * BLOCK)
            block = jnp.exp2(sbuf[at, :] - top)
            sbuf[at, :] = block
            total = total + jnp.sum(block.reshape(6, 8, TILE), axis=0)
        inverse = 1.0 / jnp.sum(total, axis=0, keepdims=True)
        for b in range(KEYS // BLOCK):
            at = slice(b * BLOCK, (b + 1) * BLOCK)
            pbuf[at, :] = (sbuf[at, :] * inverse).astype(BF16)
        out = dot(vtr[...], pbuf[...])
        acc[:, HD:] += dot(pbuf[...], ct)
        oh[g, rows, :] = out.T.astype(BF16)
        delta = jnp.sum(out.astype(BF16).astype(F32) * ct.astype(F32).T, axis=0, keepdims=True)
        dprobs = dot_nt(vmat[...], ct)
        for b in range(KEYS // BLOCK):
            at = slice(b * BLOCK, (b + 1) * BLOCK)
            pbuf[at, :] = (sbuf[at, :] * ((dprobs[at] - delta) * inverse)).astype(BF16)
        dq = dot(ktr[...], pbuf[...])
        acc[:, :HD] += dot(pbuf[...], qt)
        dqh[g, rows, :] = (dq * SCALE).T.astype(BF16)
        return carry

    lax.fori_loop(0, 2 * TILES, tile, 0)
    give(1)
    for copy in second():
        copy.wait_recv()

    source = d ^ mask
    base = d - source + 2 * N_DP
    for a in range(4):
        for b in range(4):
            piece = r2[(base - (4 * a + b)) % N_DP]
            ks[b, 16 * a : 16 * a + 16, :] = piece[:, 1024:1152]
            vs[b, 16 * a : 16 * a + 16, :] = piece[:, 1152:1280]
            for j in range(GROUP):
                qs[b, j * SHORT + 16 * a : j * SHORT + 16 * a + 16, :] = piece[
                    :, j * HD : (j + 1) * HD
                ]
    width = GROUP * SHORT
    load_c.wait()
    for b in range(4):
        for j in range(GROUP):
            at = (b * GROUP + j) * HD
            cs[b, j * SHORT : (j + 1) * SHORT, :] = scb[:, at : at + HD]
    key_row = lax.broadcasted_iota(jnp.int32, (SHORT, width), 0)
    query_row = lax.broadcasted_iota(jnp.int32, (SHORT, width), 1) & (SHORT - 1)
    key_doc = jnp.zeros((SHORT, width), jnp.int32)
    query_doc = jnp.zeros((SHORT, width), jnp.int32)
    end = jnp.int32(0)
    for k in range(4):
        end = end + dl[0, k, source]
        key_doc = key_doc + jnp.where(key_row >= end, 1, 0)
        query_doc = query_doc + jnp.where(query_row >= end, 1, 0)
    allowed = (key_doc == query_doc) & (key_row <= query_row)
    for b in range(KV_HEADS):
        qt, ct, kt, vt = qs[b], cs[b], ks[b], vs[b]
        s = jnp.where(allowed, dot_nt(kt, qt) * (SCALE * LOG2E), -1e30)
        s = jnp.exp2(s - jnp.max(s, axis=0, keepdims=True))
        probs = s * (1.0 / jnp.sum(s, axis=0, keepdims=True))
        low = probs.astype(BF16)
        out = dot(vt.astype(F32).T.astype(BF16), low)
        sdv[0, :, b * HD : (b + 1) * HD] = dot(low, ct).astype(BF16)
        delta = jnp.sum(out.astype(BF16).astype(F32) * ct.astype(F32).T, axis=0, keepdims=True)
        ds = (probs * (dot_nt(vt, ct) - delta)).astype(BF16)
        dq = dot(kt.astype(F32).T.astype(BF16), ds) * SCALE
        sdk[0, :, b * HD : (b + 1) * HD] = (dot(ds, qt) * SCALE).astype(BF16)
        out = out.T.astype(BF16)
        dq = dq.T.astype(BF16)
        for j in range(GROUP):
            at = (b * GROUP + j) * HD
            so[0, :, at : at + HD] = out[j * SHORT : (j + 1) * SHORT]
            sdq[0, :, at : at + HD] = dq[j * SHORT : (j + 1) * SHORT]
    reduce_y(1)
    reduce_z(0)
    reduce_z(1)
    arrived, own = [], []
    for g in range(2):
        for copies, here in (results(g), finals(g)):
            arrived += copies
            own += here
    for copy in own:
        copy.wait()
    for copy in arrived:
        copy.wait_recv()
    for copy in waits + first() + second() + arrived:
        copy.wait_send()
    for g in range(2):
        late = relays(g, zh, "n") + relays(g, zo, "f") + far_y(g) + sums_y(g) + [sum_z(g)]
        for copy in late:
            copy.wait_send()


def write_out(*refs):
    sources, targets, held, sems = refs[:8], refs[8:16], refs[16:24], refs[24]
    first = [
        pltpu.make_async_copy(source, block, sems.at[i])
        for i, (source, block) in enumerate(zip(sources, held))
    ]
    second = [
        pltpu.make_async_copy(block, target, sems.at[8 + i])
        for i, (block, target) in enumerate(zip(held, targets))
    ]
    for copy in first:
        copy.start()
    for copy, after in zip(first, second):
        copy.wait()
        after.start()
    for copy in second:
        copy.wait()


def per_device(*args):
    any_spec = pl.BlockSpec(memory_space=pl.ANY)
    hbm = pl.BlockSpec(memory_space=pltpu.HBM)
    vmem = pl.BlockSpec(memory_space=pltpu.VMEM)
    smem = pl.BlockSpec(memory_space=pltpu.SMEM)
    dma = pltpu.SemaphoreType.DMA
    long_query, long_key, short_query, short_key = args[0], args[1], args[5], args[6]

    args = list(args)
    args[9] = jnp.transpose(args[9], (1, 2, 0))

    def shape(like):
        return jax.ShapeDtypeStruct(like.shape, like.dtype)

    def buffer(*dims, dtype=BF16):
        return pltpu.VMEM(dims, dtype)

    results = pl.pallas_call(
        kernel,
        out_shape=(
            shape(long_query), shape(long_query), shape(long_key), shape(long_key),
            shape(short_query), shape(short_query), shape(short_key), shape(short_key),
        ),
        in_specs=[hbm] * 4 + [smem] + [hbm] * 4 + [smem] * 2,
        out_specs=(any_spec,) * 4 + (vmem,) * 4,
        scratch_shapes=[
            buffer(ROWS, 512),
            buffer(ROWS, 512),
            buffer(SHORT, 4096),
            buffer(SHORT, 512),
            buffer(SHORT, 512),
            buffer(SHORT, 4096),
            buffer(2, 2, 4, 2, 2, ROWS, HD),
            buffer(2, 2, ROWS, HD),
            buffer(2, 2, ROWS, 1024),
            buffer(2, 2, ROWS, 1024),
            buffer(2, KEYS, HD),
            buffer(2, KEYS, HD),
            buffer(2, KEYS, HD),
            buffer(2, KEYS, HD),
            buffer(2, 2, ROWS, 1024),
            buffer(2, 2, ROWS, 1024),
            buffer(KEYS, HD),
            buffer(KEYS, HD),
            buffer(HD, KEYS),
            buffer(HD, KEYS),
            buffer(3, 1, TILE, dtype=jnp.int32),
            buffer(KEYS, TILE, dtype=F32),
            buffer(KEYS, TILE),
            buffer(KEYS, 256, dtype=F32),
            buffer(2, 4, 2, 2, ROWS, 256),
            buffer(2, 3, 2, 2, ROWS, 256),
            buffer(2, 2, ROWS, 256, dtype=F32),
            buffer(2, 2, ROWS, 256),
            buffer(2, 2, ROWS, 256),
            buffer(2, 2, ROWS, 256),
            buffer(N_DP, 16, 1280),
            buffer(N_DP, 16, 1280),
            buffer(N_DP, 16, 1280),
            buffer(N_DP, 16, 1280),
            buffer(4, GROUP * SHORT, HD),
            buffer(4, GROUP * SHORT, HD),
            buffer(4, SHORT, HD),
            buffer(4, SHORT, HD),
            dma((24,)), dma((SEMS,)), dma((SEMS,)),
        ],
        compiler_params=pltpu.CompilerParams(
            collective_id=0, has_side_effects=True, vmem_limit_bytes=VMEM_LIMIT
        ),
    )(*args)
    return pl.pallas_call(
        write_out,
        out_shape=tuple(shape(result) for result in results),
        in_specs=[any_spec] * 8,
        out_specs=(hbm,) * 8,
        scratch_shapes=[buffer(*result.shape) for result in results] + [dma((16,))],
        compiler_params=pltpu.CompilerParams(vmem_limit_bytes=VMEM_LIMIT),
    )(*results)


def solution(mesh):
    wide = P("dp", "ctx", None)
    return jax.shard_map(
        per_device,
        mesh=mesh,
        in_specs=(wide,) * 4
        + (P("dp", None),)
        + (wide,) * 4
        + (P(None, "ctx", None), P("ctx", None)),
        out_specs=(wide,) * 8,
        check_vma=False,
    )
```

time: 97.4 us -> 79.2 us (0.81); the launches traced: 95.7 us -> 79 us
  local copies, waits for them, and re-layouts: 14.5 us -> 0 us
  Pallas kernels: 80.6 us -> 78.3 us
    unnamed x29 -> x0, local copies, waits for them, and re-layouts: 14.5 us -> none
    pallas_call x1, Pallas kernels: 80.6 us -> 75.5 us  [per_device(): pl.pallas_call(kernel, out_shape=(shape(long_query), shape(long_query), s...]
    pallas_call x0 -> x1, Pallas kernels: none -> 2.85 us  [per_device(): pl.pallas_call(write_out, out_shape=tuple((shape(result) for result in re...]
where the time goes in v2:
time: 79.2 us; the launch traced here: 79 us
  Pallas kernels  78.3 us (99%)
    pallas_call x1, Pallas kernels, per_device(): pl.pallas_call(kernel, out_shape=(shape(long_query), shape(long_query), s...  75.5 us
    pallas_call x1, Pallas kernels, per_device(): pl.pallas_call(write_out, out_shape=tuple((shape(result) for result in re...  2.85 us

profile of v2, /device:TPU:1, one launch (start us, length us, event | category | flops | bytes accessed | tf_op | source)
XLA Modules:
  0.0 79.0 jit_solution(9300223471448475205)
XLA Ops:
  0.6 75.5 %shard_map.170 = (bf16[1,96,4096]{2,1,0:T(8,128)(2,1)}, bf16[1,96,4096]{2,1,0:T(8,128)(2,1)}, bf16[1,96,512]{2,1,0:T(8,128)(2,1)}, bf16[1,96,512]{2,1,0:T(8,128)...) custom-call(bf16[1,96,4096]{2,1,0:T(8,128)(2,1)} %lq.1, ...), custom_call_target="tpu_custom_call" | custom-call | tf_op jit(solution)/shard_map/pallas_call | solution.py:478
  76.1 2.9 %shard_map.171 = (bf16[1,96,4096]{2,1,0:T(8,128)(2,1)}, bf16[1,96,4096]{2,1,0:T(8,128)(2,1)}, bf16[1,96,512]{2,1,0:T(8,128)(2,1)}, bf16[1,96,512]{2,1,0:T(8,128)...) custom-call(bf16[1,96,4096]{2,1,0:T(8,128)(2,1)} %get-tuple-element., ...), custom_call_target="tpu_custom_call" | custom-call | tf_op jit(solution)/shard_map/pallas_call | solution.py:531

commit v3 on v2

--- a/solution.py
+++ b/solution.py
@@ -15,12 +15,10 @@
 TILE = 256
 TILES = KEYS // TILE
 N_DP = 16
-SEMS = 96
+SEMS = 256
 VMEM_LIMIT = 62 * 1024 * 1024
-FIRST_EARLY = True
-FAR_AT = 1
-SECOND_AT = 5
-SUM_AT = 10
+PIPE = 3
+CHUNK = 384
 SCALE = HD**-0.5
 LOG2E = 1.4426950408889634
 NT = (((1,), (1,)), ((), ()))
@@ -41,7 +39,7 @@
     lq, lk, lv, lc, bo, sq, sk, sv, sc, dl, bl,
     lo, ldq, ldk, ldv, so, sdq, sdk, sdv,
     lkb, lvb, sqb, skb, svb, scb,
-    kv, kvx, qb, cb, qh, ch, oh, dqh, ob, dqb, kmat, vmat, ktr, vtr, qps, sbuf, pbuf, acc,
+    kv, kvx, qb, cb, qh, ch, oh, dqh, ob, dqb, kmat, vmat, ktr, vtr, qps, sbuf, pbuf, dbuf, delta,
     rs_s, rs_r, rz_o, rz_s, rz_r, rfin,
     st, r1, s2, r2, qs, cs, ks, vs,
     loc, sends, recvs,
@@ -65,8 +63,8 @@
 
     numbers = {}
 
-    def remote(name, src, dst, to):
-        number = numbers.setdefault(name, len(numbers))
+    def remote(name, src, dst, to, extra=0):
+        number = numbers.setdefault(name, 3 * len(numbers)) + extra
         return pltpu.make_async_remote_copy(
             src_ref=src,
             dst_ref=dst,
@@ -119,6 +117,16 @@
         kvx[g, 0] = lkb[:, other]
         kvx[g, 1] = lvb[:, other]
 
+    for copy in load_s:
+        copy.wait()
+    for a in range(4):
+        for b in range(4):
+            rows = slice(16 * a, 16 * a + 16)
+            st[4 * a + b, :, 0:1024] = sqb[rows, 1024 * b : 1024 * b + 1024]
+            st[4 * a + b, :, 1024:1152] = skb[rows, 128 * b : 128 * b + 128]
+            st[4 * a + b, :, 1152:1280] = svb[rows, 128 * b : 128 * b + 128]
+    r1[0] = st[0]
+
     pl.semaphore_wait(barrier, len(peers))
 
     waits = []
@@ -134,25 +142,29 @@
     sib_kv = [
         begin(remote(f"sib{g}", kvx.at[g], kv.at[g, zh, y, h], sib)) for g in range(2)
     ]
-    zc, own_y = [], []
-    for g in range(2):
-        mine = begin(same(f"z{g}own", kv.at[g, zh, y, h], anti))
-        sib_kv[g].wait_recv()
-        zc.append([mine, begin(same(f"z{g}sib", kv.at[g, zh, y, 1 - h], anti))])
-        own_y.append(
-            [
-                begin(same(f"up{g}", kv.at[g, zh, y], at_y(1))),
-                begin(same(f"down{g}", kv.at[g, zh, y], at_y(3))),
-            ]
-        )
-        if g == 0:
-            sib_rows = [
-                [
-                    begin(remote(f"q{k}", lq.at[0, :, wide(1 - h, k)], qb.at[k, h], sib)),
-                    begin(remote(f"c{k}", lc.at[0, :, wide(1 - h, k)], cb.at[k, h], sib)),
-                ]
-                for k in range(2)
-            ]
+    def far(g, core, name):
+        return same(f"z{g}{name}", kv.at[g, zh, y, core], anti)
+
+    def near_y(g):
+        return [
+            begin(same(f"up{g}", kv.at[g, zh, y], at_y(1))),
+            begin(same(f"down{g}", kv.at[g, zh, y], at_y(3))),
+        ]
+
+    z0 = [begin(far(0, h, "own"))]
+    sib_kv[0].wait_recv()
+    z0.append(begin(far(0, 1 - h, "sib")))
+    own_y = [near_y(0)]
+    sib_rows = [
+        [
+            begin(remote(f"q{k}", lq.at[0, :, wide(1 - h, k)], qb.at[k, h], sib)),
+            begin(remote(f"c{k}", lc.at[0, :, wide(1 - h, k)], cb.at[k, h], sib)),
+        ]
+        for k in range(2)
+    ]
+    sib_kv[1].wait_recv()
+    z1 = [begin(far(1, h, "own")), begin(far(1, 1 - h, "sib"))]
+    own_y.append(near_y(1))
 
     def first():
         return [remote(f"first{p}", st.at[p], r1.at[p], at_dp(p)) for p in range(1, N_DP)]
@@ -161,15 +173,6 @@
         return [remote(f"second{p}", s2.at[p], r2.at[p], at_dp(p)) for p in range(1, N_DP)]
 
     def begin_first():
-        for copy in load_s:
-            copy.wait()
-        for a in range(4):
-            for b in range(4):
-                rows = slice(16 * a, 16 * a + 16)
-                st[4 * a + b, :, 0:1024] = sqb[rows, 1024 * b : 1024 * b + 1024]
-                st[4 * a + b, :, 1024:1152] = skb[rows, 128 * b : 128 * b + 128]
-                st[4 * a + b, :, 1152:1280] = svb[rows, 128 * b : 128 * b + 128]
-        r1[0] = st[0]
         for copy in first():
             copy.start()
 
@@ -181,9 +184,6 @@
         r2[0] = s2[0]
         for copy in second():
             copy.start()
-
-    if FIRST_EARLY:
-        begin_first()
 
     def arrange(g):
         for copy in own_rows[g]:
@@ -216,36 +216,34 @@
 
     arrange(0)
     pass_on(own_y[0], relays(0, zh, "n"))
-    for copy in zc[0]:
+    for copy in z0:
         copy.wait_recv()
     for copy in far_y(0):
         copy.start()
+    begin_first()
     pass_on(own_y[1], relays(1, zh, "n"))
     arrange(1)
     pass_on(far_y(0), relays(0, zo, "f"))
-    for copy in zc[1]:
-        copy.wait_recv()
-    for copy in far_y(1):
-        copy.start()
-    if not FIRST_EARLY:
-        begin_first()
 
     sub = lax.broadcasted_iota(jnp.int32, (BLOCK, TILE), 0)
 
     def heads(g):
         for copy in relays(g, zh, "n") + relays(g, zo, "f"):
             copy.wait_recv()
-        kmat[...] = kv[g, :, :, :, 0].reshape(KEYS, HD)
-        vmat[...] = kv[g, :, :, :, 1].reshape(KEYS, HD)
+        for z in range(2):
+            for row in range(4):
+                to = slice(row * CHUNK + z * 192, row * CHUNK + z * 192 + 192)
+                kmat[to, :] = kv[g, z, row, :, 0].reshape(192, HD)
+                vmat[to, :] = kv[g, z, row, :, 1].reshape(192, HD)
         ktr[...] = kmat[...].T
         vtr[...] = vmat[...].T
-        acc[...] = jnp.zeros_like(acc)
+
+    def sum_y(g, k):
+        source = rs_s.at[g, (y + 1 + k) % 4]
+        return remote(f"sum{g}", source, rs_r.at[g, k], at_y(k + 1), k)
 
     def sums_y(g):
-        return [
-            remote(f"sum{g}{k}", rs_s.at[g, (y + k) % 4], rs_r.at[g, k - 1], at_y(k))
-            for k in (2, 1, 3)
-        ]
+        return [sum_y(g, k) for k in range(3)]
 
     def results(g):
         copies, own = [], []
@@ -256,15 +254,6 @@
         return copies, own
 
     def give(g):
-        for z in range(2):
-            for row in range(4):
-                part = acc[(z * 4 + row) * 192 : (z * 4 + row + 1) * 192, :]
-                rs_s[g, row, z, :, :, :HD] = (
-                    (part[:, :HD] * SCALE).astype(BF16).reshape(2, ROWS, HD)
-                )
-                rs_s[g, row, z, :, :, HD:] = part[:, HD:].astype(BF16).reshape(2, ROWS, HD)
-        for copy in sums_y(g):
-            copy.start()
         for j in range(GROUP):
             for r in range(2):
                 at = slice(j * 192 + r * ROWS, j * 192 + r * ROWS + ROWS)
@@ -310,67 +299,107 @@
         for copy in copies + own:
             copy.start()
 
-    def tile(i, carry):
-        g, t = i // TILES, i % TILES
-
-        @pl.when(i == 0)
-        def _():
-            heads(0)
-
-        @pl.when(i == FAR_AT)
-        def _():
-            pass_on(far_y(1), relays(1, zo, "f"))
-
-        @pl.when(i == SECOND_AT)
-        def _():
-            begin_second()
-
-        @pl.when(i == TILES)
-        def _():
-            give(0)
-            heads(1)
-
-        @pl.when(i == SUM_AT)
-        def _():
-            reduce_y(0)
-
-        rows = pl.ds(pl.multiple_of(t * TILE, TILE), TILE)
-        qt = qh[g, rows, :]
-        ct = ch[g, rows, :]
-        qp = qps[t % 3]
-        s = dot_nt(kmat[...], qt)
-        top = jnp.full((8, TILE), -1e30, F32)
-        for b in range(KEYS // BLOCK):
-            at = slice(b * BLOCK, (b + 1) * BLOCK)
-            block = jnp.where(sub <= qp - bo[0, b] * BLOCK, s[at] * (SCALE * LOG2E), -1e30)
-            sbuf[at, :] = block
-            top = jnp.maximum(top, jnp.max(block.reshape(6, 8, TILE), axis=0))
-        top = jnp.max(top, axis=0, keepdims=True)
-        total = jnp.zeros((8, TILE), F32)
-        for b in range(KEYS // BLOCK):
-            at = slice(b * BLOCK, (b + 1) * BLOCK)
-            block = jnp.exp2(sbuf[at, :] - top)
-            sbuf[at, :] = block
-            total = total + jnp.sum(block.reshape(6, 8, TILE), axis=0)
-        inverse = 1.0 / jnp.sum(total, axis=0, keepdims=True)
-        for b in range(KEYS // BLOCK):
-            at = slice(b * BLOCK, (b + 1) * BLOCK)
-            pbuf[at, :] = (sbuf[at, :] * inverse).astype(BF16)
-        out = dot(vtr[...], pbuf[...])
-        acc[:, HD:] += dot(pbuf[...], ct)
-        oh[g, rows, :] = out.T.astype(BF16)
-        delta = jnp.sum(out.astype(BF16).astype(F32) * ct.astype(F32).T, axis=0, keepdims=True)
-        dprobs = dot_nt(vmat[...], ct)
-        for b in range(KEYS // BLOCK):
-            at = slice(b * BLOCK, (b + 1) * BLOCK)
-            pbuf[at, :] = (sbuf[at, :] * ((dprobs[at] - delta) * inverse)).astype(BF16)
-        dq = dot(ktr[...], pbuf[...])
-        acc[:, :HD] += dot(pbuf[...], qt)
-        dqh[g, rows, :] = (dq * SCALE).T.astype(BF16)
-        return carry
-
-    lax.fori_loop(0, 2 * TILES, tile, 0)
+    def forward(g, between):
+        def steps(t, slot):
+            rows = pl.ds(pl.multiple_of(t * TILE, TILE), TILE)
+            lanes = slice(slot * TILE, (slot + 1) * TILE)
+            held = {}
+
+            def scores():
+                s = dot_nt(kmat[...], qh[g, rows, :])
+                top = jnp.full((8, TILE), -1e30, F32)
+                for b in range(KEYS // BLOCK):
+                    at = slice(b * BLOCK, (b + 1) * BLOCK)
+                    place = (b % 8) // 4 * 16 + b // 8 * 4 + b % 4
+                    seen = sub <= qps[slot] - bo[0, place] * BLOCK
+                    block = jnp.where(seen, s[at] * (SCALE * LOG2E), -1e30)
+                    sbuf[at, lanes] = block
+                    top = jnp.maximum(top, jnp.max(block.reshape(6, 8, TILE), axis=0))
+                held["top"] = jnp.max(top, axis=0, keepdims=True)
+
+            def exps():
+                total = jnp.zeros((8, TILE), F32)
+                for b in range(KEYS // BLOCK):
+                    at = slice(b * BLOCK, (b + 1) * BLOCK)
+                    block = jnp.exp2(sbuf[at, lanes] - held["top"])
+                    pbuf[at, rows] = block.astype(BF16)
+                    total = total + jnp.sum(block.reshape(6, 8, TILE), axis=0)
+                held["inverse"] = 1.0 / jnp.sum(total, axis=0, keepdims=True)
+
+            def outputs():
+                inverse = held["inverse"]
+                out = dot(vtr[...], pbuf[:, rows]) * inverse
+                oh[g, rows, :] = out.T.astype(BF16)
+                cot = ch[g, rows, :].astype(F32).T
+                low = out.astype(BF16).astype(F32)
+                delta[t] = jnp.sum(low * cot, axis=0, keepdims=True) * inverse
+                ch[g, rows, :] = (cot * inverse).T.astype(BF16)
+
+            return scores, exps, outputs
+
+        def body(i, carry):
+            @pl.when(i == 1)
+            def _():
+                between()
+
+            parts = [steps(i * PIPE + k, k) for k in range(PIPE)]
+            for step in range(PIPE + 2):
+                for stage in (2, 1, 0):
+                    if 0 <= step - stage < PIPE:
+                        parts[step - stage][stage]()
+            return carry
+
+        lax.fori_loop(0, TILES // PIPE, body, 0)
+
+    def backward(g):
+        def body(k, carry):
+            row = (y + 1 + k) % 4
+            keys = pl.ds(pl.multiple_of(row * CHUNK, CHUNK), CHUNK)
+            values = vmat[keys, :]
+            for t in range(TILES):
+                cols = slice(t * TILE, (t + 1) * TILE)
+                dprobs = dot_nt(values, ch[g, cols, :])
+                dscores = pbuf[keys, cols].astype(F32) * (dprobs - delta[t])
+                dbuf[keys, cols] = dscores.astype(BF16)
+            value_grad = dot(pbuf[keys, :], ch[g])
+            key_grad = dot(dbuf[keys, :], qh[g]) * SCALE
+            rs_s[g, row, :, :, :, HD:] = value_grad.astype(BF16).reshape(2, 2, ROWS, HD)
+            rs_s[g, row, :, :, :, :HD] = key_grad.astype(BF16).reshape(2, 2, ROWS, HD)
+
+            @pl.when(k < 3)
+            def _():
+                sum_y(g, k).start()
+
+            return carry
+
+        lax.fori_loop(0, 4, body, 0)
+
+    def query_grads(g):
+        for t in range(2):
+            cols = slice(t * 768, (t + 1) * 768)
+            dqh[g, cols, :] = (dot(ktr[...], dbuf[:, cols]) * SCALE).T.astype(BF16)
+
+    def pass_far():
+        pass_on(far_y(1), relays(1, zo, "f"))
+
+    for copy in z1:
+        copy.wait_recv()
+    for copy in far_y(1):
+        copy.start()
+    heads(0)
+    forward(0, pass_far)
+    backward(0)
+    begin_second()
+    query_grads(0)
+    give(0)
+    heads(1)
+    forward(1, lambda: None)
+    reduce_y(0)
+    backward(1)
+    query_grads(1)
     give(1)
+    reduce_z(0)
+    reduce_y(1)
     for copy in second():
         copy.wait_recv()
 
@@ -409,8 +438,8 @@
         low = probs.astype(BF16)
         out = dot(vt.astype(F32).T.astype(BF16), low)
         sdv[0, :, b * HD : (b + 1) * HD] = dot(low, ct).astype(BF16)
-        delta = jnp.sum(out.astype(BF16).astype(F32) * ct.astype(F32).T, axis=0, keepdims=True)
-        ds = (probs * (dot_nt(vt, ct) - delta)).astype(BF16)
+        sums = jnp.sum(out.astype(BF16).astype(F32) * ct.astype(F32).T, axis=0, keepdims=True)
+        ds = (probs * (dot_nt(vt, ct) - sums)).astype(BF16)
         dq = dot(kt.astype(F32).T.astype(BF16), ds) * SCALE
         sdk[0, :, b * HD : (b + 1) * HD] = (dot(ds, qt) * SCALE).astype(BF16)
         out = out.T.astype(BF16)
@@ -419,8 +448,6 @@
             at = (b * GROUP + j) * HD
             so[0, :, at : at + HD] = out[j * SHORT : (j + 1) * SHORT]
             sdq[0, :, at : at + HD] = dq[j * SHORT : (j + 1) * SHORT]
-    reduce_y(1)
-    reduce_z(0)
     reduce_z(1)
     arrived, own = [], []
     for g in range(2):
@@ -505,9 +532,10 @@
             buffer(HD, KEYS),
             buffer(HD, KEYS),
             buffer(3, 1, TILE, dtype=jnp.int32),
-            buffer(KEYS, TILE, dtype=F32),
-            buffer(KEYS, TILE),
-            buffer(KEYS, 256, dtype=F32),
+            buffer(KEYS, PIPE * TILE, dtype=F32),
+            buffer(KEYS, KEYS),
+            buffer(KEYS, KEYS),
+            buffer(TILES, 1, TILE, dtype=F32),
             buffer(2, 4, 2, 2, ROWS, 256),
             buffer(2, 3, 2, 2, ROWS, 256),
             buffer(2, 2, ROWS, 256, dtype=F32),

time: 79.2 us -> 73.3 us (0.926)
  Pallas kernels: 78.3 us -> 72.5 us
    pallas_call x1, Pallas kernels: 75.5 us -> 69.6 us  [per_device(): pl.pallas_call(kernel, out_shape=(shape(long_query), shape(long_query), s...]
where the time goes in v3:
time: 73.3 us; the launch traced here: 73.1 us
  Pallas kernels  72.5 us (99%)
    pallas_call x1, Pallas kernels, per_device(): pl.pallas_call(kernel, out_shape=(shape(long_query), shape(long_query), s...  69.6 us
    pallas_call x1, Pallas kernels, per_device(): pl.pallas_call(write_out, out_shape=tuple((shape(result) for result in re...  2.85 us

profile of v3, /device:TPU:1, one launch (start us, length us, event | category | flops | bytes accessed | tf_op | source)
XLA Modules:
  0.0 73.1 jit_solution(7642156173362980628)
XLA Ops:
  0.6 69.6 %shard_map.170 = (bf16[1,96,4096]{2,1,0:T(8,128)(2,1)}, bf16[1,96,4096]{2,1,0:T(8,128)(2,1)}, bf16[1,96,512]{2,1,0:T(8,128)(2,1)}, bf16[1,96,512]{2,1,0:T(8,128)...) custom-call(bf16[1,96,4096]{2,1,0:T(8,128)(2,1)} %lq.1, ...), custom_call_target="tpu_custom_call" | custom-call | tf_op jit(solution)/shard_map/pallas_call | solution.py:505
  70.2 2.9 %shard_map.171 = (bf16[1,96,4096]{2,1,0:T(8,128)(2,1)}, bf16[1,96,4096]{2,1,0:T(8,128)(2,1)}, bf16[1,96,512]{2,1,0:T(8,128)(2,1)}, bf16[1,96,512]{2,1,0:T(8,128)...) custom-call(bf16[1,96,4096]{2,1,0:T(8,128)(2,1)} %get-tuple-element., ...), custom_call_target="tpu_custom_call" | custom-call | tf_op jit(solution)/shard_map/pallas_call | solution.py:559

commit v4 on v3

--- a/solution.py
+++ b/solution.py
@@ -41,7 +41,7 @@
     lkb, lvb, sqb, skb, svb, scb,
     kv, kvx, qb, cb, qh, ch, oh, dqh, ob, dqb, kmat, vmat, ktr, vtr, qps, sbuf, pbuf, dbuf, delta,
     rs_s, rs_r, rz_o, rz_s, rz_r, rfin,
-    st, r1, s2, r2, qs, cs, ks, vs,
+    st, r1, s2, r2, qs, cs, ks, vs, sob, sdqb, sdkb, sdvb,
     loc, sends, recvs,
 ):
     d = lax.axis_index("dp")
@@ -398,8 +398,8 @@
     backward(1)
     query_grads(1)
     give(1)
+    reduce_y(1)
     reduce_z(0)
-    reduce_y(1)
     for copy in second():
         copy.wait_recv()
 
@@ -437,19 +437,25 @@
         probs = s * (1.0 / jnp.sum(s, axis=0, keepdims=True))
         low = probs.astype(BF16)
         out = dot(vt.astype(F32).T.astype(BF16), low)
-        sdv[0, :, b * HD : (b + 1) * HD] = dot(low, ct).astype(BF16)
+        sdvb[:, b * HD : (b + 1) * HD] = dot(low, ct).astype(BF16)
         sums = jnp.sum(out.astype(BF16).astype(F32) * ct.astype(F32).T, axis=0, keepdims=True)
         ds = (probs * (dot_nt(vt, ct) - sums)).astype(BF16)
         dq = dot(kt.astype(F32).T.astype(BF16), ds) * SCALE
-        sdk[0, :, b * HD : (b + 1) * HD] = (dot(ds, qt) * SCALE).astype(BF16)
+        sdkb[:, b * HD : (b + 1) * HD] = (dot(ds, qt) * SCALE).astype(BF16)
         out = out.T.astype(BF16)
         dq = dq.T.astype(BF16)
         for j in range(GROUP):
             at = (b * GROUP + j) * HD
-            so[0, :, at : at + HD] = out[j * SHORT : (j + 1) * SHORT]
-            sdq[0, :, at : at + HD] = dq[j * SHORT : (j + 1) * SHORT]
+            sob[:, at : at + HD] = out[j * SHORT : (j + 1) * SHORT]
+            sdqb[:, at : at + HD] = dq[j * SHORT : (j + 1) * SHORT]
+    packs = [
+        pltpu.make_async_copy(held, target.at[0], loc.at[10 + i])
+        for i, (held, target) in enumerate(((sob, so), (sdqb, sdq), (sdkb, sdk), (sdvb, sdv)))
+    ]
+    for copy in packs:
+        copy.start()
     reduce_z(1)
-    arrived, own = [], []
+    arrived, own = [], packs
     for g in range(2):
         for copies, here in (results(g), finals(g)):
             arrived += copies
@@ -488,7 +494,6 @@
 def per_device(*args):
     any_spec = pl.BlockSpec(memory_space=pl.ANY)
     hbm = pl.BlockSpec(memory_space=pltpu.HBM)
-    vmem = pl.BlockSpec(memory_space=pltpu.VMEM)
     smem = pl.BlockSpec(memory_space=pltpu.SMEM)
     dma = pltpu.SemaphoreType.DMA
     long_query, long_key, short_query, short_key = args[0], args[1], args[5], args[6]
@@ -509,7 +514,7 @@
             shape(short_query), shape(short_query), shape(short_key), shape(short_key),
         ),
         in_specs=[hbm] * 4 + [smem] + [hbm] * 4 + [smem] * 2,
-        out_specs=(any_spec,) * 4 + (vmem,) * 4,
+        out_specs=(any_spec,) * 8,
         scratch_shapes=[
             buffer(ROWS, 512),
             buffer(ROWS, 512),
@@ -550,6 +555,10 @@
             buffer(4, GROUP * SHORT, HD),
             buffer(4, SHORT, HD),
             buffer(4, SHORT, HD),
+            buffer(SHORT, 4096),
+            buffer(SHORT, 4096),
+            buffer(SHORT, 512),
+            buffer(SHORT, 512),
             dma((24,)), dma((SEMS,)), dma((SEMS,)),
         ],
         compiler_params=pltpu.CompilerParams(

time: 73.3 us -> 72.2 us (0.985)
  Pallas kernels: 72.5 us -> 71.4 us
    pallas_call x1, Pallas kernels: 69.6 us -> 68.6 us  [per_device(): pl.pallas_call(kernel, out_shape=(shape(long_query), shape(long_query), s...]
where the time goes in v4:
time: 72.2 us; the launch traced here: 72.1 us
  Pallas kernels  71.4 us (99%)
    pallas_call x1, Pallas kernels, per_device(): pl.pallas_call(kernel, out_shape=(shape(long_query), shape(long_query), s...  68.6 us
    pallas_call x1, Pallas kernels, per_device(): pl.pallas_call(write_out, out_shape=tuple((shape(result) for result in re...  2.85 us

profile of v4, /device:TPU:1, one launch (start us, length us, event | category | flops | bytes accessed | tf_op | source)
XLA Modules:
  0.0 72.1 jit_solution(7872020890735788218)
XLA Ops:
  0.6 68.6 %shard_map.170 = (bf16[1,96,4096]{2,1,0:T(8,128)(2,1)}, bf16[1,96,4096]{2,1,0:T(8,128)(2,1)}, bf16[1,96,512]{2,1,0:T(8,128)(2,1)}, bf16[1,96,512]{2,1,0:T(8,128)...) custom-call(bf16[1,96,4096]{2,1,0:T(8,128)(2,1)} %lq.1, ...), custom_call_target="tpu_custom_call" | custom-call | tf_op jit(solution)/shard_map/pallas_call | solution.py:510
  69.2 2.9 %shard_map.171 = (bf16[1,96,4096]{2,1,0:T(8,128)(2,1)}, bf16[1,96,4096]{2,1,0:T(8,128)(2,1)}, bf16[1,96,512]{2,1,0:T(8,128)(2,1)}, bf16[1,96,512]{2,1,0:T(8,128)...) custom-call(bf16[1,96,4096]{2,1,0:T(8,128)(2,1)} %get-tuple-element., ...), custom_call_target="tpu_custom_call" | custom-call | tf_op jit(solution)/shard_map/pallas_call | solution.py:568
